TPU v7x, 256 devices: a whole 4x4x8 slice. The times are simulated.
256 devices in a mesh: blk: 64 (over x_lo, z, y), rep: 4 (over x_hi, core).
Axes of the slice: x: 4 (x_hi: 2, x_lo: 2; x = x_hi * 2 + x_lo), y: 4, z: 8, core: 2. Of those that a mesh axis runs over, the one named last changes fastest.
Arguments:
- entity: bfloat16 [32768, 512], P('blk'), may hold values from -1.1953125 to 1.1953125
- relation: bfloat16 [16, 512, 512], P('rep'), may hold values from -0.25 to 0.25
- head_owner: int32 [65536, 1], P(('blk', 'rep')), may hold values from 0 to 63; in each aligned block of 256 rows (0 to 255, 256 to 511, ...) at most 8 rows name the same one
- head_row: int32 [65536], P(('blk', 'rep')), may hold values from 0 to 511
- query_rel: int32 [65536, 4], P(('blk', 'rep')), may hold values from 0 to 3
- tail_row: int32 [65536, 4], P(('blk', 'rep')), may hold values from 0 to 511
- neg_row: int32 [64, 1024], P('blk', 'rep'), may hold values from 0 to 511
Outputs:
- grad_entity: float32 [32768, 512], P('blk', 'rep')
- grad_rel: float32 [16, 512, 512], P('rep', 'blk')
Inputs may be any that keep to these rules, and one draw needn't show every extreme that they name: `head_owner`: in each aligned block of 256 rows (the heads of one group) no shard number appears more than 8 times.
All inputs are finite; a program needn't handle non-finite values.
Results may differ from a plain program's by a relative error of at most 0.0035.
Values may be sent and summed in bfloat16 or wider, within the bound.
A program may use at most 64 MiB of HBM per device.

v0:
```python
import jax
import jax.numpy as jnp
from jax import lax
from jax.sharding import PartitionSpec as P

D = 512
STOPS = 6


def shifted(block, axis, distance):
    devices = range(lax.axis_size(axis))
    route = [((i - distance) % len(devices), i) for i in devices]
    return lax.ppermute(block, axis, route)


def visit(queries, neg_block, grad_query):
    scores = jnp.dot(queries, neg_block.T, preferred_element_type=jnp.float32)
    weights = (jax.nn.sigmoid(scores) / STOPS).astype(jnp.bfloat16)
    grad_query = grad_query + jnp.dot(weights, neg_block, preferred_element_type=jnp.float32)
    block_term = jnp.einsum("qn,qd->nd", weights, queries, preferred_element_type=jnp.float32)
    return (grad_query, block_term)


def per_device(entity, relation, head_owner, head_row, query_rel, tail_row, neg_row):
    shard_count = lax.axis_size("blk")
    head_count = head_row.shape[0]
    capacity = max(2, 2 * head_count // shard_count)
    head_shard = head_owner[:, 0]
    one_hot = (head_shard[:, None] == jnp.arange(shard_count, dtype=jnp.int32)[None, :]).astype(
        jnp.int32
    )
    head_slot = jnp.sum((jnp.cumsum(one_hot, axis=0) - one_hot) * one_hot, axis=1)
    asked = jnp.full((shard_count, capacity), -1, jnp.int32).at[head_shard, head_slot].set(head_row)
    wanted = lax.all_to_all(asked, "blk", split_axis=0, concat_axis=0, tiled=True)
    served = jnp.take(entity, jnp.maximum(wanted, 0), axis=0)
    fetched, wanted = (
        lax.all_to_all(served, "blk", split_axis=0, concat_axis=0, tiled=True),
        wanted,
    )
    head_vec = fetched[head_shard, head_slot]
    products = jnp.einsum("hd,kde->khe", head_vec, relation, preferred_element_type=jnp.float32)
    rel_count = relation.shape[0]
    queries = jnp.zeros(query_rel.shape + (D,), jnp.float32)
    for rel_index in range(rel_count):
        queries = queries + jnp.where(
            (query_rel == rel_index)[:, :, None], products[rel_index][:, None, :], 0.0
        )
    queries = queries.astype(jnp.bfloat16).reshape(-1, D)
    tail_vec = jnp.take(entity, tail_row.reshape(-1), axis=0)
    pos_score = jnp.sum(queries.astype(jnp.float32) * tail_vec.astype(jnp.float32), axis=1)
    pos_weight = jax.nn.sigmoid(pos_score) - 1.0
    grad_query = pos_weight[:, None] * tail_vec.astype(jnp.float32)
    own_block = jnp.take(entity, neg_row[0], axis=0)
    fore_reach = STOPS // 2
    back_reach = STOPS - 1 - fore_reach
    neg_block = shifted(own_block, "blk", -back_reach)
    grad_query, block_grad = visit(queries, neg_block, grad_query)
    for visit_index in range(STOPS - 1):
        neg_block = shifted(neg_block, "blk", 1)
        grad_query, block_term = visit(queries, neg_block, grad_query)
        block_grad = shifted(block_grad, "blk", 1) + block_term
    own_grad = shifted(block_grad, "blk", -fore_reach)
    grad_query = grad_query.reshape(query_rel.shape + (D,))
    pair_list = []
    for rel_index in range(rel_count):
        pair_list.append(
            jnp.sum(
                jnp.where((query_rel == rel_index)[:, :, None], grad_query, 0.0), axis=1
            ).astype(jnp.bfloat16)
        )
    grad_pair = jnp.stack(pair_list)
    grad_head = jnp.einsum("khe,kde->hd", grad_pair, relation, preferred_element_type=jnp.float32)
    rel_terms = jnp.einsum("hd,khe->kde", head_vec, grad_pair, preferred_element_type=jnp.float32)
    grad_rel = lax.psum_scatter(rel_terms, "blk", scatter_dimension=1, tiled=True)
    buckets = (
        jnp.zeros((shard_count, capacity, D), jnp.float32).at[head_shard, head_slot].set(grad_head)
    )
    returned = lax.all_to_all(buckets, "blk", split_axis=0, concat_axis=0, tiled=True)
    local_grad = jnp.zeros(entity.shape, jnp.float32)
    local_grad = local_grad.at[jnp.maximum(wanted, 0).reshape(-1)].add(returned.reshape(-1, D))
    local_grad = local_grad.at[tail_row.reshape(-1)].add(
        pos_weight[:, None] * queries.astype(jnp.float32)
    )
    local_grad = local_grad.at[neg_row[0]].add(own_grad)
    grad_entity = lax.psum_scatter(local_grad, "rep", scatter_dimension=1, tiled=True)
    return (grad_entity, grad_rel)


def solution(mesh):
    placed = (
        P("blk", None),
        P("rep", None, None),
        P(("blk", "rep"), None),
        P(("blk", "rep")),
        P(("blk", "rep"), None),
        P(("blk", "rep"), None),
        P("blk", "rep"),
    )
    return jax.shard_map(
        per_device,
        mesh=mesh,
        in_specs=placed,
        out_specs=(P("blk", "rep"), P("rep", "blk", None)),
        check_vma=False,
    )
```

profile of v0, /device:TPU:16, one launch (start us, length us, event | category | flops | bytes accessed | tf_op | source)
XLA Modules:
  0.0 813.6 jit_solution(2587112022023123013)
XLA Ops:
  11.2 21.2 %scatter_fusion = s32[64,8]{0,1:T(8,128)S(1)} fusion(s32[64,8]{0,1:T(8,128)S(1)} %broadcast_in_dim.171, s32[256]{0:T(256)S(1)} %bitcast.112, s32[256]{0:T(256)} %param.10), kind=kCustom, calls=%fused_computation.4 | custom fusion | bytes 5120 | tf_op jit(solution)/shard_map/scatter | solution.py:33
  33.2 12.9 %all-to-all-start = ((s32[64,1,8]{2,1,0:T(1,128)}), s32[64,1,8]{2,1,0:T(1,128)S(1)}, u32[]{:S(2)}, u32[]{:S(2)}) async-start(s32[64,1,8]{2,1,0:T(1,128)} %copy.49), calls=%async_computation | async-start | bytes 65536 | tf_op jit(solution)/shard_map/all_to_all | solution.py:34
  49.3 5.4 all-to-all-done
  59.9 6.6 all-to-all-start.1
  69.0 10.4 %collective-permute-done.1 = bf16[256,512]{1,0:T(8,128)(2,1)} collective-permute-done((bf16[256,512]{1,0:T(8,128)(2,1)}, bf16[256,512]{1,0:T(8,128)(2,1)}, u32[]{:S(2)}, u32[]{:S(2)}) %collective-permute-start.1) | collective-permute-done | bytes 262176 | tf_op jit(solution)/shard_map/ppermute | solution.py:13
  79.4 3.9 collective-permute-start.2
  90.5 5.1 gather_fusion.2
  95.6 5.2 collective-permute-start.3
  106.2 3.0 broadcast_in_dim.180
  109.2 2.8 broadcast_in_dim.195
  111.9 3.0 broadcast_in_dim.196
  116.6 3.0 broadcast_in_dim.191
  121.3 3.0 broadcast_in_dim.186
  124.3 4.5 fusion
  141.1 4.0 collective-permute-done.4
  147.3 4.4 collective-permute-done.5
  155.3 2.9 reshape.291
  158.2 7.3 select_reduce_fusion.3
  166.5 2.8 convolution_bitcast_fusion
  169.2 5.4 copy.65
  177.0 12.1 %collective-permute-done.6 = f32[256,512]{1,0:T(8,128)S(1)} collective-permute-done((f32[256,512]{1,0:T(8,128)S(1)}, f32[256,512]{1,0:T(8,128)S(1)}, u32[]{:S(2)}, u32[]{:S(2)}) %collective-permute-start.6) | collective-permute-done | bytes 524320 | tf_op jit(solution)/shard_map/ppermute | solution.py:13
  190.2 15.9 %collective-permute-done.7 = f32[256,512]{1,0:T(8,128)S(1)} collective-permute-done((f32[256,512]{1,0:T(8,128)S(1)}, f32[256,512]{1,0:T(8,128)S(1)}, u32[]{:S(2)}, u32[]{:S(2)}) %collective-permute-start.7) | collective-permute-done | bytes 524320 | tf_op jit(solution)/shard_map/ppermute | solution.py:13
  209.8 32.2 %scatter_fusion.1 = f32[64,8,512]{2,1,0:T(8,128)} fusion(f32[64,8,512]{2,1,0:T(8,128)} %broadcast_in_dim.172, s32[256]{0:T(256)S(1)} %bitcast.113, f32[256,512]{1,0:T(8,128)} %convolution_bitcast_fusion.2), kind=kCustom, calls=%fused_computation.5 | custom fusion | bytes 1574912 | tf_op jit(solution)/shard_map/scatter | solution.py:76
  242.0 19.3 %all-to-all-start.2 = ((f32[64,8,512]{2,1,0:T(8,128)}), f32[64,8,512]{2,1,0:T(8,128)}, u32[]{:S(2)}, u32[]{:S(2)}) async-start(f32[64,8,512]{2,1,0:T(8,128)} %scatter_fusion.1), calls=%async_computation.2 | async-start | bytes 2097152 | tf_op jit(solution)/shard_map/all_to_all | solution.py:78
  265.7 19.4 %collective-permute-done.9 = f32[256,512]{1,0:T(8,128)S(1)} collective-permute-done((f32[256,512]{1,0:T(8,128)S(1)}, f32[256,512]{1,0:T(8,128)S(1)}, u32[]{:S(2)}, u32[]{:S(2)}) %collective-permute-start.9) | collective-permute-done | bytes 524320 | tf_op jit(solution)/shard_map/ppermute | solution.py:13
  285.2 9.5 %collective-permute-start.10 = (f32[256,512]{1,0:T(8,128)S(1)}, f32[256,512]{1,0:T(8,128)S(1)}, u32[]{:S(2)}, u32[]{:S(2)}) collective-permute-start(f32[256,512]{1,0:T(8,128)S(1)} %add.204), channel_id=1, source_target_pairs={{252,0},{0,4},{4,8},{8,12},{12,16},{16,20},{20,24},{24,28},{28,32}... | collective-permute-start | bytes 1572872 | tf_op jit(solution)/shard_map/ppermute | solution.py:13
  295.2 7.8 collective-permute-done.10
  303.9 11.9 %collective-permute-start.11 = (f32[256,512]{1,0:T(8,128)}, f32[256,512]{1,0:T(8,128)}, u32[]{:S(2)}, u32[]{:S(2)}) collective-permute-start(f32[256,512]{1,0:T(8,128)} %add.205), channel_id=1, source_target_pairs={{12,0},{16,4},{20,8},{24,12},{28,16},{32,20},{36,24},{40,28},{44,3... | collective-permute-start | bytes 1572872 | tf_op jit(solution)/shard_map/ppermute | solution.py:13
  315.7 5.4 scatter_custom_fusion.2
  321.1 9.4 %scatter_custom_fusion.3 = f32[512,512]{1,0:T(8,128)} fusion(f32[512,512]{1,0:T(8,128)} %scatter_custom_fusion.2, s32[1024]{0:T(1024)S(1)} %bitcast.124, bf16[1024,512]{1,0:T(8,128)(2,1)S(1)} %get-tuple-element.15, f32[1024]{0:T(1024)S(1)} %divide_add_fusion), kind=kCustom, calls=%fused_computation.13 | custom fusion | flops 1572864 | bytes 2101248 | tf_op jit(solution)/shard_map/scatter-add | solution.py:81
  330.5 4.8 scatter_fusion.2
  336.6 467.8 %all-reduce.3.cloned.1.call-done = f32[4,512,512]{2,0,1:T(4,128)} async-done(((f32[4,512,512]{2,0,1:T(4,128)}), f32[4,512,512]{2,0,1:T(4,128)}) %all-reduce.3.cloned.1.call-update) | async-done | bytes 4194320
  (153 shorter events, 64.3 us)
Async XLA Ops:
  8.0 94.8 %copy-start = (bf16[4,512,512]{2,1,0:T(8,128)(2,1)S(1)}, bf16[4,512,512]{2,1,0:T(8,128)(2,1)}, u32[]{:S(2)}) copy-start(bf16[4,512,512]{2,1,0:T(8,128)(2,1)} %param.8) | copy-start | bytes 6291460
  8.0 38.1 %copy-start.27 = (s32[1,256]{1,0:T(1,128)S(1)}, s32[1,256]{1,0:T(1,128)}, u32[]{:S(2)}) copy-start(s32[1,256]{1,0:T(1,128)} %param.13) | copy-start | bytes 3076
  8.0 38.6 %copy-start.1 = (bf16[512,512]{1,0:T(8,128)(2,1)S(1)}, bf16[512,512]{1,0:T(8,128)(2,1)}, u32[]{:S(2)}) copy-start(bf16[512,512]{1,0:T(8,128)(2,1)} %param.7) | copy-start | bytes 1572868
  11.2 37.2 %copy-start.21 = (s32[256,4]{0,1:T(4,128)S(1)}, s32[256,4]{0,1:T(4,128)}, u32[]{:S(2)}) copy-start(s32[256,4]{0,1:T(4,128)} %param.12) | copy-start | bytes 12292
  33.2 21.6 %all-to-all-start = ((s32[64,1,8]{2,1,0:T(1,128)}), s32[64,1,8]{2,1,0:T(1,128)S(1)}, u32[]{:S(2)}, u32[]{:S(2)}) async-start(s32[64,1,8]{2,1,0:T(1,128)} %copy.49), calls=%async_computation | async-start | bytes 65536 | tf_op jit(solution)/shard_map/all_to_all | solution.py:34
  47.9 19.9 %collective-permute-start = (bf16[256,512]{1,0:T(8,128)(2,1)S(1)}, bf16[256,512]{1,0:T(8,128)(2,1)}, u32[]{:S(2)}, u32[]{:S(2)}) collective-permute-start(bf16[256,512]{1,0:T(8,128)(2,1)S(1)} %broadcast_select_fusion), channel_id=1, source_target_pairs={{8,0},{12,4},{16,8},{20,12},{24,16},{28,20},{32,24},{36,28},{40,32... | collective-permute-start | bytes 786440 | tf_op jit(solution)/shard_map/ppermute | solution.py:13
  58.2 10.8 %copy-start.22 = (s32[1024,1]{0,1:T(1,128)S(1)}, s32[1024,1]{0,1:T(1,128)}, u32[]{:S(2)}) copy-start(s32[1024,1]{0,1:T(1,128)} %reshape.289) | copy-start | bytes 12292
  59.9 40.9 %all-to-all-start.1 = ((bf16[64,8,512]{2,1,0:T(8,128)(2,1)}), bf16[64,8,512]{2,1,0:T(8,128)(2,1)S(1)}, u32[]{:S(2)}, u32[]{:S(2)}) async-start(bf16[64,8,512]{2,1,0:T(8,128)(2,1)} %bitcast_select_fusion), calls=%async_computation.1 | async-start | bytes 1048576 | tf_op jit(solution)/shard_map/all_to_all | solution.py:37
  66.5 738.0 %all-reduce.3.cloned.1.call-start = ((), (), s32[]{:S(2)}) async-start(), calls=%async_computation.5 | async-start | bytes 8388608
  67.8 11.6 %collective-permute-start.1 = (bf16[256,512]{1,0:T(8,128)(2,1)}, bf16[256,512]{1,0:T(8,128)(2,1)}, u32[]{:S(2)}, u32[]{:S(2)}) collective-permute-start(bf16[256,512]{1,0:T(8,128)(2,1)} %collective-permute-done), channel_id=1, source_target_pairs={{252,0},{0,4},{4,8},{8,12},{12,16},{16,20},{20,24},{24,28},{28,32}... | collective-permute-start | bytes 786440 | tf_op jit(solution)/shard_map/ppermute | solution.py:13
  79.4 16.1 %collective-permute-start.2 = (bf16[256,512]{1,0:T(8,128)(2,1)}, bf16[256,512]{1,0:T(8,128)(2,1)}, u32[]{:S(2)}, u32[]{:S(2)}) collective-permute-start(bf16[256,512]{1,0:T(8,128)(2,1)} %collective-permute-done.1), channel_id=1, source_target_pairs={{252,0},{0,4},{4,8},{8,12},{12,16},{16,20},{20,24},{24,28},{28,32}... | collective-permute-start | bytes 786440 | tf_op jit(solution)/shard_map/ppermute | solution.py:13
  95.6 42.4 %collective-permute-start.3 = (bf16[256,512]{1,0:T(8,128)(2,1)}, bf16[256,512]{1,0:T(8,128)(2,1)}, u32[]{:S(2)}, u32[]{:S(2)}) collective-permute-start(bf16[256,512]{1,0:T(8,128)(2,1)} %collective-permute-done.2), channel_id=1, source_target_pairs={{252,0},{0,4},{4,8},{8,12},{12,16},{16,20},{20,24},{24,28},{28,32}... | collective-permute-start | bytes 786440 | tf_op jit(solution)/shard_map/ppermute | solution.py:13
  138.0 7.1 collective-permute-start.4
  139.6 5.6 copy-start.9
  145.1 6.5 collective-permute-start.5
  147.3 5.7 copy-start.2
  174.7 14.5 %copy-start.6 = (bf16[1024,256]{1,0:T(8,128)(2,1)S(1)}, bf16[1024,256]{1,0:T(8,128)(2,1)}, u32[]{:S(2)}) copy-start(bf16[1024,256]{1,0:T(8,128)(2,1)} %copy-done.5) | copy-start | bytes 1572868
  174.7 15.1 %copy-start.11 = (bf16[1024,256]{1,0:T(8,128)(2,1)S(1)}, bf16[1024,256]{1,0:T(8,128)(2,1)}, u32[]{:S(2)}) copy-start(bf16[1024,256]{1,0:T(8,128)(2,1)} %copy-done.10) | copy-start | bytes 1572868
  176.3 12.9 %collective-permute-start.6 = (f32[256,512]{1,0:T(8,128)S(1)}, f32[256,512]{1,0:T(8,128)S(1)}, u32[]{:S(2)}, u32[]{:S(2)}) collective-permute-start(f32[256,512]{1,0:T(8,128)S(1)} %fusion.51), channel_id=1, source_target_pairs={{252,0},{0,4},{4,8},{8,12},{12,16},{16,20},{20,24},{24,28},{28,32}... | collective-permute-start | bytes 1572872 | tf_op jit(solution)/shard_map/ppermute | solution.py:13
  189.6 17.4 %copy-start.14 = (bf16[256,512]{1,0:T(8,128)(2,1)S(1)}, bf16[256,512]{1,0:T(8,128)(2,1)}, u32[]{:S(2)}) copy-start(bf16[256,512]{1,0:T(8,128)(2,1)} %copy-done.13) | copy-start | bytes 786436
  189.7 17.4 %copy-start.16 = (bf16[256,512]{1,0:T(8,128)(2,1)S(1)}, bf16[256,512]{1,0:T(8,128)(2,1)}, u32[]{:S(2)}) copy-start(bf16[256,512]{1,0:T(8,128)(2,1)} %copy-done.15) | copy-start | bytes 786436
  189.7 17.4 %copy-start.18 = (bf16[256,512]{1,0:T(8,128)(2,1)S(1)}, bf16[256,512]{1,0:T(8,128)(2,1)}, u32[]{:S(2)}) copy-start(bf16[256,512]{1,0:T(8,128)(2,1)} %copy-done.17) | copy-start | bytes 786436
  189.7 17.4 %copy-start.20 = (bf16[256,512]{1,0:T(8,128)(2,1)S(1)}, bf16[256,512]{1,0:T(8,128)(2,1)}, u32[]{:S(2)}) copy-start(bf16[256,512]{1,0:T(8,128)(2,1)} %copy-done.19) | copy-start | bytes 786436
  189.7 16.5 %collective-permute-start.7 = (f32[256,512]{1,0:T(8,128)S(1)}, f32[256,512]{1,0:T(8,128)S(1)}, u32[]{:S(2)}, u32[]{:S(2)}) collective-permute-start(f32[256,512]{1,0:T(8,128)S(1)} %convolution_add_fusion), channel_id=1, source_target_pairs={{252,0},{0,4},{4,8},{8,12},{12,16},{16,20},{20,24},{24,28},{28,32}... | collective-permute-start | bytes 1572872 | tf_op jit(solution)/shard_map/ppermute | solution.py:13
  207.1 55.8 %collective-permute-start.8 = (f32[256,512]{1,0:T(8,128)}, f32[256,512]{1,0:T(8,128)}, u32[]{:S(2)}, u32[]{:S(2)}) collective-permute-start(f32[256,512]{1,0:T(8,128)} %add.202), channel_id=1, source_target_pairs={{252,0},{0,4},{4,8},{8,12},{12,16},{16,20},{20,24},{24,28},{28,32}... | collective-permute-start | bytes 1572872 | tf_op jit(solution)/shard_map/ppermute | solution.py:13
  242.0 73.7 %all-to-all-start.2 = ((f32[64,8,512]{2,1,0:T(8,128)}), f32[64,8,512]{2,1,0:T(8,128)}, u32[]{:S(2)}, u32[]{:S(2)}) async-start(f32[64,8,512]{2,1,0:T(8,128)} %scatter_fusion.1), calls=%async_computation.2 | async-start | bytes 2097152 | tf_op jit(solution)/shard_map/all_to_all | solution.py:78
  261.3 544.7 %reduce-scatter.2.cloned.1.call-start = ((), (), s32[]{:S(2)}) async-start(), calls=%async_computation.4 | async-start | bytes 1310720 | tf_op jit(solution)/shard_map/reduce_scatter | solution.py:85
  264.0 30.7 %copy-start.4 = (bf16[1024,256]{1,0:T(8,128)(2,1)S(1)}, bf16[1024,256]{1,0:T(8,128)(2,1)}, u32[]{:S(2)}) copy-start(bf16[1024,256]{1,0:T(8,128)(2,1)} %copy-done.3) | copy-start | bytes 1572868
  264.0 21.1 %collective-permute-start.9 = (f32[256,512]{1,0:T(8,128)S(1)}, f32[256,512]{1,0:T(8,128)S(1)}, u32[]{:S(2)}, u32[]{:S(2)}) collective-permute-start(f32[256,512]{1,0:T(8,128)S(1)} %add.203), channel_id=1, source_target_pairs={{252,0},{0,4},{4,8},{8,12},{12,16},{16,20},{20,24},{24,28},{28,32}... | collective-permute-start | bytes 1572872 | tf_op jit(solution)/shard_map/ppermute | solution.py:13
  285.2 17.8 %collective-permute-start.10 = (f32[256,512]{1,0:T(8,128)S(1)}, f32[256,512]{1,0:T(8,128)S(1)}, u32[]{:S(2)}, u32[]{:S(2)}) collective-permute-start(f32[256,512]{1,0:T(8,128)S(1)} %add.204), channel_id=1, source_target_pairs={{252,0},{0,4},{4,8},{8,12},{12,16},{16,20},{20,24},{24,28},{28,32}... | collective-permute-start | bytes 1572872 | tf_op jit(solution)/shard_map/ppermute | solution.py:13
  303.8 26.7 %copy-start.24 = (s32[256,1]{0,1:T(1,128)S(1)}, s32[256,1]{0,1:T(1,128)}, u32[]{:S(2)}) copy-start(s32[256,1]{0,1:T(1,128)} %copy-done.23) | copy-start | bytes 3076
  303.9 26.7 %collective-permute-start.11 = (f32[256,512]{1,0:T(8,128)}, f32[256,512]{1,0:T(8,128)}, u32[]{:S(2)}, u32[]{:S(2)}) collective-permute-start(f32[256,512]{1,0:T(8,128)} %add.205), channel_id=1, source_target_pairs={{12,0},{16,4},{20,8},{24,12},{28,16},{32,20},{36,24},{40,28},{44,3... | collective-permute-start | bytes 1572872 | tf_op jit(solution)/shard_map/ppermute | solution.py:13
  (14 other events, 27.3 us)
Sparse Core Ops, SparseCore 0:
  174.8 629.6 all-reduce.2
Sparse Core Ops, SparseCore 1:
  335.4 37.8 reduce-scatter.1
where the time goes:
time: 824 us; the launch traced here: 814 us
  waiting for transfers between devices  547 us (66%)
  local copies, waits for them, and re-layouts  109 us (13%)
  starting transfers between devices  74.1 us (9%)
  other arithmetic  40.5 us (5%)
  matrix products  25.7 us (3%)
  between operations  17 us (2%)
    unnamed x3, waiting for transfers between devices  468 us
    ppermute x12, waiting for transfers between devices, shifted(): return lax.ppermute(block, axis, route)  74.1 us
    ppermute x12, starting transfers between devices, shifted(): return lax.ppermute(block, axis, route)  35.3 us
    scatter x1, local copies, waits for them, and re-layouts, per_device(): jnp.zeros((shard_count, capacity, D), jnp.float32).at[head_shard, head_slot]  32.2 us
    broadcast_in_dim x12, local copies, waits for them, and re-layouts, per_device(): jnp.where((query_rel == rel_index)[:, :, None], products[rel_index][:, No...  22.9 us
    scatter x1, local copies, waits for them, and re-layouts, per_device(): jnp.full((shard_count, capacity), -1, jnp.int32).at[head_shard, head_slot]  21.2 us
    all_to_all x1, starting transfers between devices, per_device(): lax.all_to_all(buckets, 'blk', split_axis=0, concat_axis=0, tiled=True)  19.3 us
  transfers between devices with their start and end apart: 17, of which 9 were waited for; matrix products, arithmetic and copies ran while one was open for 15% of the time, Pallas kernels for 0%

commit v1 on v0

v1 whole, which is shorter than its diff:
```python
import functools

import jax
import jax.numpy as jnp
from jax import lax
from jax.experimental import pallas as pl
from jax.experimental.pallas import tpu as pltpu
from jax.sharding import PartitionSpec as P

D = 512
STOPS = 6
NBLK, NY, NZ, NX, NREP = 64, 4, 8, 2, 4
OFFS = (0, 1, -1, 3, 2, -2)
MESH = pl.DeviceIdType.MESH
F32, BF16, I32 = jnp.float32, jnp.bfloat16, jnp.int32
NT = (((1,), (1,)), ((), ()))
TN = (((0,), (0,)), ((), ()))


def iota(shape, dim):
    return lax.broadcasted_iota(I32, shape, dim)


def hot(mask):
    return jnp.where(mask, 1.0, 0.0).astype(BF16)


def mm(a, b):
    return jnp.dot(a, b, preferred_element_type=F32)


def mm_nt(a, b):
    return lax.dot_general(a, b, NT, preferred_element_type=F32)


def mm_tn(a, b):
    return lax.dot_general(a, b, TN, preferred_element_type=F32)


def two_parts(value):
    high = value.astype(BF16)
    return high, (value - high.astype(F32)).astype(BF16)


def kernel(
    ent, rel, cols, rows, out_e, out_r,
    asked, wanted, wanted2, w_row, served, fetched, blocks, tails, head, head_t, head_p,
    prod, query, pos_w, grad_q, pair, pair_p, term, term_own, term_s, term_r, back_s, back_r,
    rel_f, rel_s, rel_y, rz_f, rz_s, rz_r, rx_s, rx_r, loc, loc_s, loc_r,
    a2a_sem, nb_sem, gt_sem, x_sem, y_sem, z_sem, rep_sem,
):
    b, r = lax.axis_index("blk"), lax.axis_index("rep")
    y, z, xl = lax.rem(b, NY), lax.rem(lax.div(b, NY), NZ), lax.div(b, NY * NZ)
    xp = 1 - xl
    other_x = lax.rem(b + NY * NZ, NBLK)

    def send(src, dst, s_sem, r_sem, blk, rep):
        copy = pltpu.make_async_remote_copy(
            src_ref=src, dst_ref=dst, send_sem=s_sem, recv_sem=r_sem, device_id=(blk, rep), device_id_type=MESH
        )
        copy.start()
        return copy

    def wait_all(ref, sem):
        pltpu.make_async_copy(ref, ref, sem).wait()

    def to_all(src, dst, s_sem, r_sem):
        def step(k, carry):
            peer = lax.rem(b + k, NBLK)
            send(src(peer), dst, s_sem, r_sem, peer, r)
            return carry

        lax.fori_loop(1, NBLK, step, 0)

    def rows16(ref):
        return lambda s: ref.at[pl.ds(pl.multiple_of(s * 16, 16), 16)]

    barrier = pltpu.get_barrier_semaphore()

    def greet(k, carry):
        pl.semaphore_signal(barrier, inc=1, device_id=(lax.rem(b + k, NBLK), r), device_id_type=MESH)
        return carry

    lax.fori_loop(1, NBLK, greet, 0)
    for d in range(1, NREP):
        pl.semaphore_signal(barrier, inc=1, device_id=(b, lax.rem(r + d, NREP)), device_id_type=MESH)

    owner_row, owner_col = rows[0:1, :], cols[:, 0:1]
    in_shard = iota((NBLK, 256), 0) == owner_row
    shard_hot = hot(in_shard)
    before = mm(shard_hot, hot(iota((256, 256), 0) < iota((256, 256), 1)))
    slot_row = jnp.sum(jnp.where(in_shard, before, 0.0), axis=0, keepdims=True)
    place_row = owner_row * 16 + slot_row.astype(I32)
    of_head = iota((256, 128), 1) == owner_col
    before = mm(hot(iota((256, 256), 1) < iota((256, 256), 0)), hot(of_head))
    slot_col = jnp.sum(jnp.where(of_head, before, 0.0), axis=1, keepdims=True).astype(I32)
    place_col = owner_col * 16 + slot_col
    named = cols[:, 1:2] + 1
    lane = iota((256, 128), 1)
    digits = jnp.where(lane == slot_col, named >> 5, 0) + jnp.where(lane == slot_col + 64, named & 31, 0)
    requests = mm(shard_hot, digits.astype(F32).astype(BF16))
    for s in range(NBLK):
        asked[s] = requests[s : s + 1, :]
    blocks[0] = mm(hot(iota((256, D), 1) == cols[:, 10:11]), ent[...]).astype(BF16)

    pl.semaphore_wait(barrier, NBLK - 1 + NREP - 1)
    to_all(lambda s: asked.at[s], wanted.at[b], a2a_sem.at[0], a2a_sem.at[1])
    wanted[b] = asked[b]
    for j in range(2):
        tails[j] = mm(hot(iota((256, D), 1) == cols[:, 6 + j : 7 + j]), ent[...]).astype(BF16)
    wait_all(wanted.at[pl.ds(0, NBLK - 1)], a2a_sem.at[1])

    for s in range(NBLK):
        wanted2[s : s + 1, :] = wanted[s]
    spread = mm(hot(iota((1024, NBLK), 0) >> 4 == iota((1024, NBLK), 1)), wanted2[...].astype(BF16))
    k_of, lane = iota((1024, 128), 0) & 7, iota((1024, 128), 1)
    spread = jnp.where(lane == k_of, spread * 32.0, jnp.where(lane == k_of + 64, spread, 0.0))
    w_row[...] = mm_nt(jnp.ones((8, 128), BF16), spread.astype(BF16)).astype(I32) - 1
    w_col = jnp.sum(spread, axis=1, keepdims=True).astype(I32) - 1
    first_half = (iota((256, 256), 0) >> 3 & 1) == 0
    for t in range(4):
        whole = mm(hot(iota((256, D), 1) == w_col[t * 256 : (t + 1) * 256]), ent[...])
        served[t * 256 : (t + 1) * 256] = jnp.where(first_half, whole[:, :256], whole[:, 256:]).astype(BF16)
    mine = pl.ds(pl.multiple_of(b * 16, 16), 16)
    to_all(rows16(served), fetched.at[mine], a2a_sem.at[2], a2a_sem.at[3])
    block_out = []
    for n in range(1, STOPS):
        visitor = lax.rem(b + OFFS[n] + NBLK, NBLK)
        block_out.append(send(blocks.at[0], blocks.at[n], nb_sem.at[n - 1], nb_sem.at[4 + n], visitor, r))
    fetched[mine] = served[mine]
    for j in range(2, 4):
        tails[j] = mm(hot(iota((256, D), 1) == cols[:, 6 + j : 7 + j]), ent[...]).astype(BF16)
    wait_all(fetched.at[pl.ds(0, (NBLK - 1) * 16)], a2a_sem.at[3])
    for h in range(2):
        picked = hot(iota((256, 1024), 1) == place_col + 8 * h)
        head[:, h * 256 : (h + 1) * 256] = mm(picked, fetched[...]).astype(BF16)

    for k in range(4):
        prod[k] = mm(head[...], rel[k])

    def query_rows(t, carry):
        at = pl.ds(pl.multiple_of(t * 16, 16), 16)
        kind = cols[at, :]
        for j in range(4):
            q = prod[0, at, :]
            for k in range(1, 4):
                q = jnp.where(kind[:, 2 + j : 3 + j] == k, prod[k, at, :], q)
            q = q.astype(BF16)
            query[j, at, :] = q
            tail = tails[j, at, :].astype(F32)
            score = jnp.sum(q.astype(F32) * tail, axis=1, keepdims=True)
            weight = jax.nn.sigmoid(score) - 1.0
            grad_q[j, at, :] = weight * tail
            pos_w[j, at, :] = jnp.broadcast_to(weight, (16, 128))
        return carry

    lax.fori_loop(0, 16, query_rows, 0)

    c = iota((D, D), 0)
    natural = (c >> 3 & 1) * 256 + (c >> 4 & 7) * 32 + (c >> 7) * 8 + (c & 7)
    head_t[...] = mm_nt(hot(iota((D, D), 1) == natural), head[...]).astype(BF16)
    head_out = send(head_t, head_p, x_sem.at[0], x_sem.at[1], other_x, r)

    term_out = []
    for n in range(STOPS):
        if n:
            block_out[n - 1].wait_recv()
        acc = term if n else term_own
        acc[...] = jnp.zeros_like(acc)

        def visit(j, carry, n=n, acc=acc):
            q, block = query[j], blocks[n]
            weight = (jax.nn.sigmoid(mm_nt(q, block)) / STOPS).astype(BF16)
            grad_q[j] += mm(weight, block)
            acc[...] += mm_tn(weight, q)
            return carry

        lax.fori_loop(0, 4, visit, 0)
        if n:
            term_s[n - 1] = term[...].astype(BF16)
            owner = lax.rem(b - OFFS[n] + NBLK, NBLK)
            term_out.append(send(term_s.at[n - 1], term_r.at[n - 1], gt_sem.at[n - 1], gt_sem.at[4 + n], owner, r))

    def pair_rows(t, carry):
        at = pl.ds(pl.multiple_of(t * 16, 16), 16)
        kind = cols[at, :]
        for k in range(4):
            total = jnp.zeros((16, D), F32)
            for j in range(4):
                total += jnp.where(kind[:, 2 + j : 3 + j] == k, grad_q[j, at, :], 0.0)
            pair[k, at, :] = total.astype(BF16)
        return carry

    lax.fori_loop(0, 16, pair_rows, 0)
    pair_out = send(pair.at[pl.ds(2 * xp, 2)], pair_p, x_sem.at[2], x_sem.at[3], other_x, r)

    grad_head = mm_nt(pair[0], rel[0])
    for k in range(1, 4):
        grad_head += mm_nt(pair[k], rel[k])
    grad_head = grad_head.astype(BF16)
    for t in range(4):
        q = iota((256, 256), 0) + t * 256
        whole = mm(hot(q - (q >> 3 & 1) * 8 == place_row), grad_head)
        back_s[t * 256 : (t + 1) * 256] = jnp.where(first_half, whole[:, :256], whole[:, 256:]).astype(BF16)
    to_all(rows16(back_s), back_r.at[mine], a2a_sem.at[4], a2a_sem.at[5])
    back_r[mine] = back_s[mine]

    head_out.wait_recv()
    pair_out.wait_recv()
    for k in range(2):
        rel_f[k] = mm(head_t[...], pair[2 * xl + k]) + mm(head_p[...], pair_p[k])
        rel_s[k] = rel_f[k].astype(BF16)
    y_out = []
    for d in range(1, NY):
        yp = lax.rem(y + d, NY)
        part = rel_s.at[:, pl.ds(pl.multiple_of(yp * 128, 128), 128), :]
        y_out.append(send(part, rel_y.at[d - 1], y_sem.at[d - 1], y_sem.at[2 + d], b - y + yp, r))

    for j in range(4):
        onto = hot(iota((D, 256), 0) == rows[6 + j : 7 + j, :])
        high, low = two_parts(pos_w[j, :, 0:1] * query[j].astype(F32))
        part = mm(onto, high) + mm(onto, low)
        for c in range(4):
            loc[c] = part[:, c * 128 : (c + 1) * 128] if j == 0 else loc[c] + part[:, c * 128 : (c + 1) * 128]
    wait_all(back_r.at[pl.ds(0, (NBLK - 1) * 16)], a2a_sem.at[5])
    lanes = iota((D, 1024), 1)
    for h in range(2):
        onto = hot((iota((D, 1024), 0) == w_row[0:1, :]) & ((lanes >> 3 & 1) == h))
        part = mm(onto, back_r[...])
        for c in range(2):
            loc[2 * h + c] += part[:, c * 128 : (c + 1) * 128]
    total = term_own[...]
    for n in range(STOPS - 1):
        term_out[n].wait_recv()
        total += term_r[n].astype(F32)
    onto = hot(iota((D, 256), 0) == rows[10:11, :])
    high, low = two_parts(total)
    part = mm(onto, high) + mm(onto, low)
    for c in range(4):
        loc[c] += part[:, c * 128 : (c + 1) * 128]
        loc_s[c] = loc[c].astype(BF16)
    rep_out = []
    for d in range(1, NREP):
        rp = lax.rem(r + d, NREP)
        rep_out.append(send(loc_s.at[rp], loc_r.at[d - 1], rep_sem.at[d - 1], rep_sem.at[2 + d], b, rp))

    rz_f[...] = rel_f[:, pl.ds(pl.multiple_of(y * 128, 128), 128), :]
    for d in range(1, NY):
        y_out[d - 1].wait_recv()
        rz_f[...] += rel_y[d - 1].astype(F32)
    rz_s[...] = rz_f[...].astype(BF16)
    z_out = []
    for d in range(1, NZ):
        zp = lax.rem(z + d, NZ)
        part = rz_s.at[:, pl.ds(pl.multiple_of(zp * 16, 16), 16), :]
        z_out.append(send(part, rz_r.at[d - 1], z_sem.at[d - 1], z_sem.at[6 + d], b + (zp - z) * NY, r))

    total = loc[r]
    for d in range(1, NREP):
        rep_out[d - 1].wait_recv()
        total += loc_r[d - 1].astype(F32)
    out_e[...] = total

    total = rz_f[:, pl.ds(pl.multiple_of(z * 16, 16), 16), :]
    for d in range(1, NZ):
        z_out[d - 1].wait_recv()
        total += rz_r[d - 1].astype(F32)
    for x in range(NX):
        rx_s[x] = total[:, x * 8 : (x + 1) * 8, :]
    x_out = send(rx_s.at[xp], rx_r, x_sem.at[4], x_sem.at[5], other_x, r)
    for k in range(2):
        out_r[2 * xl + k] = rx_s[xl, k]
    x_out.wait_recv()
    for k in range(2):
        out_r[2 * xp + k] = rx_r[k]

    for copy in (*block_out, head_out, *term_out, pair_out, *y_out, *rep_out, *z_out, x_out):
        copy.wait_send()
    wait_all(asked.at[pl.ds(0, NBLK - 1)], a2a_sem.at[0])
    wait_all(served.at[pl.ds(0, (NBLK - 1) * 16)], a2a_sem.at[2])
    wait_all(back_s.at[pl.ds(0, (NBLK - 1) * 16)], a2a_sem.at[4])


def per_device(entity, relation, head_owner, head_row, query_rel, tail_row, neg_row):
    cols = jnp.concatenate([head_owner, head_row[:, None], query_rel, tail_row, neg_row.T], axis=1)
    rows = cols.T
    vmem = pl.BlockSpec(memory_space=pltpu.VMEM)
    dma = pltpu.SemaphoreType.DMA
    scratch = [
        pltpu.VMEM((NBLK, 1, 128), F32),
        pltpu.VMEM((NBLK, 1, 128), F32),
        pltpu.VMEM((NBLK, 128), F32),
        pltpu.VMEM((8, 1024), I32),
        pltpu.VMEM((1024, 256), BF16),
        pltpu.VMEM((1024, 256), BF16),
        pltpu.VMEM((STOPS, 256, D), BF16),
        pltpu.VMEM((4, 256, D), BF16),
        pltpu.VMEM((256, D), BF16),
        pltpu.VMEM((D, 256), BF16),
        pltpu.VMEM((D, 256), BF16),
        pltpu.VMEM((4, 256, D), F32),
        pltpu.VMEM((4, 256, D), BF16),
        pltpu.VMEM((4, 256, 128), F32),
        pltpu.VMEM((4, 256, D), F32),
        pltpu.VMEM((4, 256, D), BF16),
        pltpu.VMEM((2, 256, D), BF16),
        pltpu.VMEM((256, D), F32),
        pltpu.VMEM((256, D), F32),
        pltpu.VMEM((STOPS - 1, 256, D), BF16),
        pltpu.VMEM((STOPS - 1, 256, D), BF16),
        pltpu.VMEM((1024, 256), BF16),
        pltpu.VMEM((1024, 256), BF16),
        pltpu.VMEM((2, D, D), F32),
        pltpu.VMEM((2, D, D), BF16),
        pltpu.VMEM((NY - 1, 2, 128, D), BF16),
        pltpu.VMEM((2, 128, D), F32),
        pltpu.VMEM((2, 128, D), BF16),
        pltpu.VMEM((NZ - 1, 2, 16, D), BF16),
        pltpu.VMEM((NX, 2, 8, D), F32),
        pltpu.VMEM((2, 8, D), F32),
        pltpu.VMEM((4, D, 128), F32),
        pltpu.VMEM((4, D, 128), BF16),
        pltpu.VMEM((NREP - 1, D, 128), BF16),
        dma((6,)),
        dma((10,)),
        dma((10,)),
        dma((6,)),
        dma((6,)),
        dma((14,)),
        dma((6,)),
    ]
    return pl.pallas_call(
        kernel,
        out_shape=(jax.ShapeDtypeStruct((D, 128), F32), jax.ShapeDtypeStruct((4, 8, D), F32)),
        in_specs=[vmem] * 4,
        out_specs=(vmem, vmem),
        scratch_shapes=scratch,
        compiler_params=pltpu.CompilerParams(
            collective_id=0, has_side_effects=True, vmem_limit_bytes=50 * 2**20
        ),
        name="rescal_step",
    )(entity, relation, cols, rows)


def solution(mesh):
    placed = (
        P("blk", None),
        P("rep", None, None),
        P(("blk", "rep"), None),
        P(("blk", "rep")),
        P(("blk", "rep"), None),
        P(("blk", "rep"), None),
        P("blk", "rep"),
    )
    return jax.shard_map(
        per_device,
        mesh=mesh,
        in_specs=placed,
        out_specs=(P("blk", "rep"), P("rep", "blk", None)),
        check_vma=False,
    )
```

time: 824 us -> 109 us (0.13); the launches traced: 814 us -> 108 us
  waiting for transfers between devices: 547 us -> 0 us
  local copies, waits for them, and re-layouts: 109 us -> 6.29 us
  Pallas kernels: 0 us -> 101 us
  starting transfers between devices: 74.1 us -> 0 us
  other arithmetic: 40.5 us -> 0 us
  matrix products: 25.7 us -> 0 us
  between operations: 17 us -> 0.65 us
    unnamed x3 -> x0, waiting for transfers between devices: 468 us -> none
    pallas_call x0 -> x1, Pallas kernels: none -> 101 us  [per_device(): pl.pallas_call(kernel, out_shape=(jax.ShapeDtypeStruct((D, 128), F32), ja...]
    ppermute x12 -> x0, waiting for transfers between devices: 74.1 us -> none  [shifted(): return lax.ppermute(block, axis, route)]
    scatter x2 -> x0, local copies, waits for them, and re-layouts: 53.5 us -> none  [the longest x1 32.2 us: per_device(): jnp.zeros((shard_count, capacity, D), jnp.float32).at[head_shard, head_slot]]
    all_to_all x3 -> x0, starting transfers between devices: 38.8 us -> none  [the longest x1 19.3 us: per_device(): lax.all_to_all(buckets, 'blk', split_axis=0, concat_axis=0, tiled=True)]
    ppermute x12 -> x0, starting transfers between devices: 35.3 us -> none  [shifted(): return lax.ppermute(block, axis, route)]
    dot_general x21 -> x0, matrix products: 25.7 us -> none  [the longest x6 8.66 us: visit(): jnp.dot(weights, neg_block, preferred_element_type=jnp.float32)]
    broadcast_in_dim x16 -> x0, local copies, waits for them, and re-layouts: 25.4 us -> none  [the longest x12 22.9 us: per_device(): jnp.where((query_rel == rel_index)[:, :, None], products[rel_index][:, No...]
  transfers between devices with their start and end apart: 17 -> 0, of which waited for: 9 -> 0; matrix products, arithmetic and copies ran while one was open for 15% -> 0% of each run, Pallas kernels for 0% -> 0%
where the time goes in v1:
time: 109 us; the launch traced here: 108 us
  Pallas kernels  101 us (93%)
  local copies, waits for them, and re-layouts  6.29 us (6%)
    pallas_call x1, Pallas kernels, per_device(): pl.pallas_call(kernel, out_shape=(jax.ShapeDtypeStruct((D, 128), F32), ja...  101 us
    unnamed x6, local copies, waits for them, and re-layouts  3.96 us
    concatenate x2, local copies, waits for them, and re-layouts, per_device(): jnp.concatenate([head_owner, head_row[:, None], query_rel, tail_row, neg_...  2.33 us

profile of v1, /device:TPU:16, one launch (start us, length us, event | category | flops | bytes accessed | tf_op | source)
XLA Modules:
  0.0 107.7 jit_solution(1298208054047319704)
XLA Ops:
  0.6 2.2 %concatenate.3 = s32[256,11]{0,1:T(8,128)S(1)} concatenate(s32[256,1]{0,1:T(1,128)} %param.9, s32[256,1]{0,1:T(1,128)} %bitcast.4, s32[256,4]{0,1:T(4,128)} %param.11, s32[256,4]{0,1:T(4,128)} %param.12, s32[256,1]{0,1:T(1,128)} %bitcast.5), dimensions={1} | concatenate | bytes 22528 | tf_op jit(solution)/shard_map/concatenate | solution.py:285
  2.8 0.1 copy.9.cols
  3.0 0.0 copy-start
  3.0 1.6 %copy-done = bf16[4,512,512]{2,1,0:T(8,128)(2,1)S(1)} copy-done((bf16[4,512,512]{2,1,0:T(8,128)(2,1)S(1)}, bf16[4,512,512]{2,1,0:T(8,128)(2,1)}, u32[]{:S(2)}) %copy-start) | copy-done | bytes 2097176
  4.6 0.0 copy-start.1
  4.6 1.0 copy-done.1
  5.6 100.8 %rescal_step.1 = (f32[512,128]{1,0:T(8,128)S(1)}, f32[4,8,512]{2,1,0:T(8,128)S(1)}) custom-call(bf16[512,512]{1,0:T(8,128)(2,1)S(1)} %copy-done.1, bf16[4,512,512]{2,1,0:T(8,128)(2,1)S(1)} %copy-done, s32[256,11]{1,0:T(8,128)S(1)} %copy.9.cols, s32[11,256]{1,0:T(8,128)S(1)} %bitcast.3), custom_call_target="tpu_custom_call" | custom-call | tf_op jit(solution)/shard_map/rescal_step/pallas_call | solution.py:332
  106.4 0.7 copy.12
  107.1 0.6 copy.13
Async XLA Ops:
  3.0 1.6 %copy-start = (bf16[4,512,512]{2,1,0:T(8,128)(2,1)S(1)}, bf16[4,512,512]{2,1,0:T(8,128)(2,1)}, u32[]{:S(2)}) copy-start(bf16[4,512,512]{2,1,0:T(8,128)(2,1)} %rel.1) | copy-start | bytes 6291460
  4.6 1.0 copy-start.1

commit v2 on v1

--- a/solution.py
+++ b/solution.py
@@ -10,7 +10,7 @@
 D = 512
 STOPS = 6
 NBLK, NY, NZ, NX, NREP = 64, 4, 8, 2, 4
-OFFS = (0, 1, -1, 3, 2, -2)
+OFFS = (0, 1, -1, 2, -2, 3)
 MESH = pl.DeviceIdType.MESH
 F32, BF16, I32 = jnp.float32, jnp.bfloat16, jnp.int32
 NT = (((1,), (1,)), ((), ()))
@@ -43,23 +43,29 @@
 
 
 def kernel(
-    ent, rel, cols, rows, out_e, out_r,
-    asked, wanted, wanted2, w_row, served, fetched, blocks, tails, head, head_t, head_p,
-    prod, query, pos_w, grad_q, pair, pair_p, term, term_own, term_s, term_r, back_s, back_r,
+    ent_h, rel_h, owner_h, row_h, kind_h, tail_h, neg_h, out_e, out_r,
+    ent, rel, owner_v, row_v, kind_v, tail_v, neg_v, rows, cols, asked, wanted, wanted2, w_row, served, fetched, blocks, relay, tails, head, head_t, head_p,
+    prod, query, pos_w, grad_q, weights, pair, pair_p, term_own, term_s, term_r, term_f, relay_s, relay_r, back_s, back_r,
     rel_f, rel_s, rel_y, rz_f, rz_s, rz_r, rx_s, rx_r, loc, loc_s, loc_r,
-    a2a_sem, nb_sem, gt_sem, x_sem, y_sem, z_sem, rep_sem,
+    in_sem, a2a_sem, nb_sem, gt_sem, hop_sem, x_sem, y_sem, z_sem, rep_sem,
 ):
     b, r = lax.axis_index("blk"), lax.axis_index("rep")
     y, z, xl = lax.rem(b, NY), lax.rem(lax.div(b, NY), NZ), lax.div(b, NY * NZ)
     xp = 1 - xl
     other_x = lax.rem(b + NY * NZ, NBLK)
 
-    def send(src, dst, s_sem, r_sem, blk, rep):
-        copy = pltpu.make_async_remote_copy(
+    def remote(src, dst, s_sem, r_sem, blk, rep):
+        return pltpu.make_async_remote_copy(
             src_ref=src, dst_ref=dst, send_sem=s_sem, recv_sem=r_sem, device_id=(blk, rep), device_id_type=MESH
         )
+
+    def send(*copy_args):
+        copy = remote(*copy_args)
         copy.start()
         return copy
+
+    def block(n):
+        return blocks.at[pl.ds(n * 256, 256)]
 
     def wait_all(ref, sem):
         pltpu.make_async_copy(ref, ref, sem).wait()
@@ -84,6 +90,25 @@
     lax.fori_loop(1, NBLK, greet, 0)
     for d in range(1, NREP):
         pl.semaphore_signal(barrier, inc=1, device_id=(b, lax.rem(r + d, NREP)), device_id_type=MESH)
+
+    index_in = []
+    for n, (src, dst) in enumerate(
+        ((owner_h, owner_v), (row_h, row_v), (kind_h, kind_v), (tail_h, tail_v), (neg_h, neg_v))
+    ):
+        index_in.append(pltpu.make_async_copy(src, dst, in_sem.at[n]))
+    ent_in = pltpu.make_async_copy(ent_h, ent, in_sem.at[5])
+    rel_in = pltpu.make_async_copy(rel_h, rel, in_sem.at[6])
+    for copy in (*index_in, ent_in, rel_in):
+        copy.start()
+    for copy in index_in:
+        copy.wait()
+    rows[...] = jnp.zeros_like(rows)
+    rows[0:1, :] = owner_v[...]
+    rows[1:2, :] = row_v[...]
+    rows[2:6, :] = kind_v[...]
+    rows[6:10, :] = tail_v[...]
+    rows[10:11, :] = neg_v[...]
+    cols[...] = jnp.transpose(rows[...])
 
     owner_row, owner_col = rows[0:1, :], cols[:, 0:1]
     in_shard = iota((NBLK, 256), 0) == owner_row
@@ -101,13 +126,28 @@
     requests = mm(shard_hot, digits.astype(F32).astype(BF16))
     for s in range(NBLK):
         asked[s] = requests[s : s + 1, :]
-    blocks[0] = mm(hot(iota((256, D), 1) == cols[:, 10:11]), ent[...]).astype(BF16)
+    ent_in.wait()
+    block(0)[...] = mm(hot(iota((256, D), 1) == cols[:, 10:11]), ent[...]).astype(BF16)
+    rel_in.wait()
 
     pl.semaphore_wait(barrier, NBLK - 1 + NREP - 1)
     to_all(lambda s: asked.at[s], wanted.at[b], a2a_sem.at[0], a2a_sem.at[1])
     wanted[b] = asked[b]
+
+    plane_up, plane_down = lax.rem(b + NY, NBLK), lax.rem(b + NBLK - NY, NBLK)
+    up_out = remote(block(0), relay.at[0], hop_sem.at[0], hop_sem.at[1], plane_up, r)
+    down_out = remote(block(0), relay.at[1], hop_sem.at[2], hop_sem.at[3], plane_down, r)
+    pl.when(y >= 1)(up_out.start)
+    pl.when(y <= 1)(down_out.start)
+    block_out, block_far = [], []
+    for n in range(1, STOPS):
+        visitor = b - y + lax.rem(y + OFFS[n] + NY, NY)
+        sems = nb_sem.at[n - 1], nb_sem.at[4 + n]
+        block_out.append(remote(block(0), block(n), *sems, visitor, r))
+        block_far.append(remote(relay.at[0 if OFFS[n] > 0 else 1], block(n), *sems, visitor, r))
+        pl.when((y + OFFS[n] >= 0) & (y + OFFS[n] < NY))(block_out[n - 1].start)
     for j in range(2):
-        tails[j] = mm(hot(iota((256, D), 1) == cols[:, 6 + j : 7 + j]), ent[...]).astype(BF16)
+        tails[j * 256 : (j + 1) * 256] = mm(hot(iota((256, D), 1) == cols[:, 6 + j : 7 + j]), ent[...]).astype(BF16)
     wait_all(wanted.at[pl.ds(0, NBLK - 1)], a2a_sem.at[1])
 
     for s in range(NBLK):
@@ -123,13 +163,13 @@
         served[t * 256 : (t + 1) * 256] = jnp.where(first_half, whole[:, :256], whole[:, 256:]).astype(BF16)
     mine = pl.ds(pl.multiple_of(b * 16, 16), 16)
     to_all(rows16(served), fetched.at[mine], a2a_sem.at[2], a2a_sem.at[3])
-    block_out = []
+    fetched[mine] = served[mine]
+    pl.when(y >= 1)(up_out.wait_recv)
+    pl.when(y <= 1)(down_out.wait_recv)
     for n in range(1, STOPS):
-        visitor = lax.rem(b + OFFS[n] + NBLK, NBLK)
-        block_out.append(send(blocks.at[0], blocks.at[n], nb_sem.at[n - 1], nb_sem.at[4 + n], visitor, r))
-    fetched[mine] = served[mine]
+        pl.when((y + OFFS[n] < 0) | (y + OFFS[n] >= NY))(block_far[n - 1].start)
     for j in range(2, 4):
-        tails[j] = mm(hot(iota((256, D), 1) == cols[:, 6 + j : 7 + j]), ent[...]).astype(BF16)
+        tails[j * 256 : (j + 1) * 256] = mm(hot(iota((256, D), 1) == cols[:, 6 + j : 7 + j]), ent[...]).astype(BF16)
     wait_all(fetched.at[pl.ds(0, (NBLK - 1) * 16)], a2a_sem.at[3])
     for h in range(2):
         picked = hot(iota((256, 1024), 1) == place_col + 8 * h)
@@ -142,19 +182,20 @@
         at = pl.ds(pl.multiple_of(t * 16, 16), 16)
         kind = cols[at, :]
         for j in range(4):
+            to = pl.ds(pl.multiple_of(j * 256 + t * 16, 16), 16)
             q = prod[0, at, :]
             for k in range(1, 4):
                 q = jnp.where(kind[:, 2 + j : 3 + j] == k, prod[k, at, :], q)
             q = q.astype(BF16)
-            query[j, at, :] = q
-            tail = tails[j, at, :].astype(F32)
+            query[to, :] = q
+            tail = tails[to, :].astype(F32)
             score = jnp.sum(q.astype(F32) * tail, axis=1, keepdims=True)
             weight = jax.nn.sigmoid(score) - 1.0
-            grad_q[j, at, :] = weight * tail
-            pos_w[j, at, :] = jnp.broadcast_to(weight, (16, 128))
+            grad_q[to, :] = weight * tail
+            pos_w[to, :] = jnp.broadcast_to(weight, (16, 128))
         return carry
 
-    lax.fori_loop(0, 16, query_rows, 0)
+    lax.fori_loop(0, 16, query_rows, 0, unroll=2)
 
     c = iota((D, D), 0)
     natural = (c >> 3 & 1) * 256 + (c >> 4 & 7) * 32 + (c >> 7) * 8 + (c & 7)
@@ -165,21 +206,21 @@
     for n in range(STOPS):
         if n:
             block_out[n - 1].wait_recv()
-        acc = term if n else term_own
-        acc[...] = jnp.zeros_like(acc)
-
-        def visit(j, carry, n=n, acc=acc):
-            q, block = query[j], blocks[n]
-            weight = (jax.nn.sigmoid(mm_nt(q, block)) / STOPS).astype(BF16)
-            grad_q[j] += mm(weight, block)
-            acc[...] += mm_tn(weight, q)
-            return carry
-
-        lax.fori_loop(0, 4, visit, 0)
-        if n:
-            term_s[n - 1] = term[...].astype(BF16)
-            owner = lax.rem(b - OFFS[n] + NBLK, NBLK)
-            term_out.append(send(term_s.at[n - 1], term_r.at[n - 1], gt_sem.at[n - 1], gt_sem.at[4 + n], owner, r))
+        met = slice(n * 256, (n + 1) * 256)
+        weights[:, met] = (jax.nn.sigmoid(mm_nt(query[...], block(n)[...])) * (1.0 / STOPS)).astype(BF16)
+        term = mm_tn(weights[:, met], query[...])
+        if n == 0:
+            term_own[...] = term
+        else:
+            term_s[n - 1] = term.astype(BF16)
+            via = b - y + lax.rem(y - OFFS[n] + NY, NY)
+            term_out.append(send(term_s.at[n - 1], term_r.at[n - 1], gt_sem.at[n - 1], gt_sem.at[4 + n], via, r))
+        for upto, since in ((4, 0), (STOPS, 4)):
+            if n == upto - 1:
+                met = slice(since * 256, upto * 256)
+                for j in range(4):
+                    at = slice(j * 256, (j + 1) * 256)
+                    grad_q[at, :] += mm(weights[at, met], blocks[met, :])
 
     def pair_rows(t, carry):
         at = pl.ds(pl.multiple_of(t * 16, 16), 16)
@@ -187,11 +228,11 @@
         for k in range(4):
             total = jnp.zeros((16, D), F32)
             for j in range(4):
-                total += jnp.where(kind[:, 2 + j : 3 + j] == k, grad_q[j, at, :], 0.0)
+                total += jnp.where(kind[:, 2 + j : 3 + j] == k, grad_q[pl.ds(pl.multiple_of(j * 256 + t * 16, 16), 16), :], 0.0)
             pair[k, at, :] = total.astype(BF16)
         return carry
 
-    lax.fori_loop(0, 16, pair_rows, 0)
+    lax.fori_loop(0, 16, pair_rows, 0, unroll=2)
     pair_out = send(pair.at[pl.ds(2 * xp, 2)], pair_p, x_sem.at[2], x_sem.at[3], other_x, r)
 
     grad_head = mm_nt(pair[0], rel[0])
@@ -218,10 +259,29 @@
 
     for j in range(4):
         onto = hot(iota((D, 256), 0) == rows[6 + j : 7 + j, :])
-        high, low = two_parts(pos_w[j, :, 0:1] * query[j].astype(F32))
+        high, low = two_parts(pos_w[j * 256 : (j + 1) * 256, 0:1] * query[j * 256 : (j + 1) * 256, :].astype(F32))
         part = mm(onto, high) + mm(onto, low)
         for c in range(4):
             loc[c] = part[:, c * 128 : (c + 1) * 128] if j == 0 else loc[c] + part[:, c * 128 : (c + 1) * 128]
+
+    term_f[...] = jnp.zeros_like(term_f)
+    for n in range(1, STOPS):
+        term_out[n - 1].wait_recv()
+
+        def own(n=n):
+            term_own[...] += term_r[n - 1].astype(F32)
+
+        def other(n=n):
+            term_f[0 if OFFS[n] > 0 else 1] += term_r[n - 1].astype(F32)
+
+        pl.when((y + OFFS[n] >= 0) & (y + OFFS[n] < NY))(own)
+        pl.when((y + OFFS[n] < 0) | (y + OFFS[n] >= NY))(other)
+    relay_s[...] = term_f[...].astype(BF16)
+    low_out = remote(relay_s.at[0], relay_r.at[0], hop_sem.at[4], hop_sem.at[5], plane_down, r)
+    high_out = remote(relay_s.at[1], relay_r.at[1], hop_sem.at[6], hop_sem.at[7], plane_up, r)
+    pl.when(y >= 1)(low_out.start)
+    pl.when(y <= 1)(high_out.start)
+
     wait_all(back_r.at[pl.ds(0, (NBLK - 1) * 16)], a2a_sem.at[5])
     lanes = iota((D, 1024), 1)
     for h in range(2):
@@ -229,20 +289,6 @@
         part = mm(onto, back_r[...])
         for c in range(2):
             loc[2 * h + c] += part[:, c * 128 : (c + 1) * 128]
-    total = term_own[...]
-    for n in range(STOPS - 1):
-        term_out[n].wait_recv()
-        total += term_r[n].astype(F32)
-    onto = hot(iota((D, 256), 0) == rows[10:11, :])
-    high, low = two_parts(total)
-    part = mm(onto, high) + mm(onto, low)
-    for c in range(4):
-        loc[c] += part[:, c * 128 : (c + 1) * 128]
-        loc_s[c] = loc[c].astype(BF16)
-    rep_out = []
-    for d in range(1, NREP):
-        rp = lax.rem(r + d, NREP)
-        rep_out.append(send(loc_s.at[rp], loc_r.at[d - 1], rep_sem.at[d - 1], rep_sem.at[2 + d], b, rp))
 
     rz_f[...] = rel_f[:, pl.ds(pl.multiple_of(y * 128, 128), 128), :]
     for d in range(1, NY):
@@ -255,11 +301,26 @@
         part = rz_s.at[:, pl.ds(pl.multiple_of(zp * 16, 16), 16), :]
         z_out.append(send(part, rz_r.at[d - 1], z_sem.at[d - 1], z_sem.at[6 + d], b + (zp - z) * NY, r))
 
-    total = loc[r]
+    def from_above():
+        low_out.wait_recv()
+        term_own[...] += relay_r[0].astype(F32)
+
+    def from_below():
+        high_out.wait_recv()
+        term_own[...] += relay_r[1].astype(F32)
+
+    pl.when(y >= 1)(from_above)
+    pl.when(y <= 1)(from_below)
+    onto = hot(iota((D, 256), 0) == rows[10:11, :])
+    high, low = two_parts(term_own[...])
+    part = mm(onto, high) + mm(onto, low)
+    for c in range(4):
+        loc[c] += part[:, c * 128 : (c + 1) * 128]
+        loc_s[c] = loc[c].astype(BF16)
+    rep_out = []
     for d in range(1, NREP):
-        rep_out[d - 1].wait_recv()
-        total += loc_r[d - 1].astype(F32)
-    out_e[...] = total
+        rp = lax.rem(r + d, NREP)
+        rep_out.append(send(loc_s.at[rp], loc_r.at[d - 1], rep_sem.at[d - 1], rep_sem.at[2 + d], b, rp))
 
     total = rz_f[:, pl.ds(pl.multiple_of(z * 16, 16), 16), :]
     for d in range(1, NZ):
@@ -268,12 +329,22 @@
     for x in range(NX):
         rx_s[x] = total[:, x * 8 : (x + 1) * 8, :]
     x_out = send(rx_s.at[xp], rx_r, x_sem.at[4], x_sem.at[5], other_x, r)
+    total = loc[r]
+    for d in range(1, NREP):
+        rep_out[d - 1].wait_recv()
+        total += loc_r[d - 1].astype(F32)
+    out_e[...] = total
+
     for k in range(2):
         out_r[2 * xl + k] = rx_s[xl, k]
     x_out.wait_recv()
     for k in range(2):
         out_r[2 * xp + k] = rx_r[k]
 
+    pl.when(y >= 1)(up_out.wait_send)
+    pl.when(y <= 1)(down_out.wait_send)
+    pl.when(y >= 1)(low_out.wait_send)
+    pl.when(y <= 1)(high_out.wait_send)
     for copy in (*block_out, head_out, *term_out, pair_out, *y_out, *rep_out, *z_out, x_out):
         copy.wait_send()
     wait_all(asked.at[pl.ds(0, NBLK - 1)], a2a_sem.at[0])
@@ -282,32 +353,43 @@
 
 
 def per_device(entity, relation, head_owner, head_row, query_rel, tail_row, neg_row):
-    cols = jnp.concatenate([head_owner, head_row[:, None], query_rel, tail_row, neg_row.T], axis=1)
-    rows = cols.T
     vmem = pl.BlockSpec(memory_space=pltpu.VMEM)
     dma = pltpu.SemaphoreType.DMA
     scratch = [
+        pltpu.VMEM((D, D), BF16),
+        pltpu.VMEM((4, D, D), BF16),
+        pltpu.VMEM((1, 256), I32),
+        pltpu.VMEM((1, 256), I32),
+        pltpu.VMEM((4, 256), I32),
+        pltpu.VMEM((4, 256), I32),
+        pltpu.VMEM((1, 256), I32),
+        pltpu.VMEM((128, 256), I32),
+        pltpu.VMEM((256, 128), I32),
         pltpu.VMEM((NBLK, 1, 128), F32),
         pltpu.VMEM((NBLK, 1, 128), F32),
         pltpu.VMEM((NBLK, 128), F32),
         pltpu.VMEM((8, 1024), I32),
         pltpu.VMEM((1024, 256), BF16),
         pltpu.VMEM((1024, 256), BF16),
-        pltpu.VMEM((STOPS, 256, D), BF16),
-        pltpu.VMEM((4, 256, D), BF16),
+        pltpu.VMEM((STOPS * 256, D), BF16),
+        pltpu.VMEM((2, 256, D), BF16),
+        pltpu.VMEM((1024, D), BF16),
         pltpu.VMEM((256, D), BF16),
         pltpu.VMEM((D, 256), BF16),
         pltpu.VMEM((D, 256), BF16),
         pltpu.VMEM((4, 256, D), F32),
-        pltpu.VMEM((4, 256, D), BF16),
-        pltpu.VMEM((4, 256, 128), F32),
-        pltpu.VMEM((4, 256, D), F32),
+        pltpu.VMEM((1024, D), BF16),
+        pltpu.VMEM((1024, 128), F32),
+        pltpu.VMEM((1024, D), F32),
+        pltpu.VMEM((1024, STOPS * 256), BF16),
         pltpu.VMEM((4, 256, D), BF16),
         pltpu.VMEM((2, 256, D), BF16),
         pltpu.VMEM((256, D), F32),
-        pltpu.VMEM((256, D), F32),
         pltpu.VMEM((STOPS - 1, 256, D), BF16),
         pltpu.VMEM((STOPS - 1, 256, D), BF16),
+        pltpu.VMEM((2, 256, D), F32),
+        pltpu.VMEM((2, 256, D), BF16),
+        pltpu.VMEM((2, 256, D), BF16),
         pltpu.VMEM((1024, 256), BF16),
         pltpu.VMEM((1024, 256), BF16),
         pltpu.VMEM((2, D, D), F32),
@@ -321,9 +403,11 @@
         pltpu.VMEM((4, D, 128), F32),
         pltpu.VMEM((4, D, 128), BF16),
         pltpu.VMEM((NREP - 1, D, 128), BF16),
+        dma((7,)),
         dma((6,)),
         dma((10,)),
         dma((10,)),
+        dma((8,)),
         dma((6,)),
         dma((6,)),
         dma((14,)),
@@ -332,14 +416,14 @@
     return pl.pallas_call(
         kernel,
         out_shape=(jax.ShapeDtypeStruct((D, 128), F32), jax.ShapeDtypeStruct((4, 8, D), F32)),
-        in_specs=[vmem] * 4,
+        in_specs=[pl.BlockSpec(memory_space=pl.ANY)] * 7,
         out_specs=(vmem, vmem),
         scratch_shapes=scratch,
         compiler_params=pltpu.CompilerParams(
-            collective_id=0, has_side_effects=True, vmem_limit_bytes=50 * 2**20
+            collective_id=0, has_side_effects=True, vmem_limit_bytes=61 * 2**20
         ),
         name="rescal_step",
-    )(entity, relation, cols, rows)
+    )(entity, relation, head_owner.T, head_row[None, :], query_rel.T, tail_row.T, neg_row)
 
 
 def solution(mesh):

time: 109 us -> 102 us (0.936)
  Pallas kernels: 101 us -> 97.7 us
  local copies, waits for them, and re-layouts: 6.29 us -> 3.14 us
    pallas_call x1, Pallas kernels: 101 us -> 97.7 us  [per_device(): pl.pallas_call(kernel, out_shape=(jax.ShapeDtypeStruct((D, 128), F32), ja...]
    concatenate x2 -> x0, local copies, waits for them, and re-layouts: 2.33 us -> none  [per_device(): jnp.concatenate([head_owner, head_row[:, None], query_rel, tail_row, neg_...]
    unnamed x6 -> x2, local copies, waits for them, and re-layouts: 3.96 us -> 3.14 us
where the time goes in v2:
time: 102 us; the launch traced here: 101 us
  Pallas kernels  97.7 us (96%)
  local copies, waits for them, and re-layouts  3.14 us (3%)
    pallas_call x1, Pallas kernels, per_device(): pl.pallas_call(kernel, out_shape=(jax.ShapeDtypeStruct((D, 128), F32), ja...  97.7 us
    unnamed x2, local copies, waits for them, and re-layouts  3.14 us

profile of v2, /device:TPU:16, one launch (start us, length us, event | category | flops | bytes accessed | tf_op | source)
XLA Modules:
  0.0 101.4 jit_solution(11765115473668596297)
XLA Ops:
  0.6 97.7 %rescal_step.1 = (f32[512,128]{1,0:T(8,128)}, f32[4,8,512]{2,1,0:T(8,128)}) custom-call(bf16[512,512]{1,0:T(8,128)(2,1)} %ent_h.1, bf16[4,512,512]{2,1,0:T(8,128)(2,1)} %rel_h.1, s32[1,256]{1,0:T(1,128)} %bitcast.6, s32[1,256]{1,0:T(1,128)} %bitcast.7, s32[4,256]{1,0:T(4,128)} %bitcast.4, s32[4,256]{1,0:T(4,128)} %bitcast.5, s32[1,256]{1,0:T(1,128)} %neg_h.1), custom_call_target="tpu_custom_call" | custom-call | tf_op jit(solution)/shard_map/rescal_step/pallas_call | solution.py:416
  98.3 1.7 %copy.11 = f32[512,128]{1,0:T(8,128)} copy(f32[512,128]{1,0:T(8,128)} %get-tuple-element.4) | data formatting | bytes 524288
  100.0 1.5 %copy.12 = f32[4,8,512]{2,1,0:T(8,128)} copy(f32[4,8,512]{2,1,0:T(8,128)} %get-tuple-element.5) | data formatting | bytes 131072

commit v3 on v2

--- a/solution.py
+++ b/solution.py
@@ -46,8 +46,8 @@
     ent_h, rel_h, owner_h, row_h, kind_h, tail_h, neg_h, out_e, out_r,
     ent, rel, owner_v, row_v, kind_v, tail_v, neg_v, rows, cols, asked, wanted, wanted2, w_row, served, fetched, blocks, relay, tails, head, head_t, head_p,
     prod, query, pos_w, grad_q, weights, pair, pair_p, term_own, term_s, term_r, term_f, relay_s, relay_r, back_s, back_r,
-    rel_f, rel_s, rel_y, rz_f, rz_s, rz_r, rx_s, rx_r, loc, loc_s, loc_r,
-    in_sem, a2a_sem, nb_sem, gt_sem, hop_sem, x_sem, y_sem, z_sem, rep_sem,
+    rel_f, rel_s, rel_y, rel_z, ya_f, ya_s, ya_r, zb_f, zb_s, zb_r, rx_s, rx_r, loc, loc_s, loc_r,
+    in_sem, a2a_sem, nb_sem, gt_sem, hop_sem, x_sem, y_sem, z_sem, y2_sem, z2_sem, rep_sem,
 ):
     b, r = lax.axis_index("blk"), lax.axis_index("rep")
     y, z, xl = lax.rem(b, NY), lax.rem(lax.div(b, NY), NZ), lax.div(b, NY * NZ)
@@ -246,23 +246,29 @@
     to_all(rows16(back_s), back_r.at[mine], a2a_sem.at[4], a2a_sem.at[5])
     back_r[mine] = back_s[mine]
 
-    head_out.wait_recv()
-    pair_out.wait_recv()
-    for k in range(2):
-        rel_f[k] = mm(head_t[...], pair[2 * xl + k]) + mm(head_p[...], pair_p[k])
-        rel_s[k] = rel_f[k].astype(BF16)
-    y_out = []
-    for d in range(1, NY):
-        yp = lax.rem(y + d, NY)
-        part = rel_s.at[:, pl.ds(pl.multiple_of(yp * 128, 128), 128), :]
-        y_out.append(send(part, rel_y.at[d - 1], y_sem.at[d - 1], y_sem.at[2 + d], b - y + yp, r))
-
     for j in range(4):
         onto = hot(iota((D, 256), 0) == rows[6 + j : 7 + j, :])
         high, low = two_parts(pos_w[j * 256 : (j + 1) * 256, 0:1] * query[j * 256 : (j + 1) * 256, :].astype(F32))
         part = mm(onto, high) + mm(onto, low)
         for c in range(4):
             loc[c] = part[:, c * 128 : (c + 1) * 128] if j == 0 else loc[c] + part[:, c * 128 : (c + 1) * 128]
+
+    head_out.wait_recv()
+    pair_out.wait_recv()
+    for k in (1, 0):
+        total = (mm(head_t[...], pair[2 * xl + k]) + mm(head_p[...], pair_p[k])).reshape(NY, NZ, 16, D)
+        rel_f[k] = total
+        rel_s[k] = total.astype(BF16)
+        if k:
+            zb_in = []
+            for d in range(1, NZ):
+                zp = lax.rem(z + d, NZ)
+                to = b + (zp - z) * NY
+                zb_in.append(send(rel_s.at[1, :, zp], rel_z.at[d - 1], z_sem.at[d - 1], z_sem.at[6 + d], to, r))
+    ya_in = []
+    for d in range(1, NY):
+        yp = lax.rem(y + d, NY)
+        ya_in.append(send(rel_s.at[0, yp], rel_y.at[d - 1], y_sem.at[d - 1], y_sem.at[2 + d], b - y + yp, r))
 
     term_f[...] = jnp.zeros_like(term_f)
     for n in range(1, STOPS):
@@ -290,16 +296,27 @@
         for c in range(2):
             loc[2 * h + c] += part[:, c * 128 : (c + 1) * 128]
 
-    rz_f[...] = rel_f[:, pl.ds(pl.multiple_of(y * 128, 128), 128), :]
+    total = rel_f[0, y]
     for d in range(1, NY):
-        y_out[d - 1].wait_recv()
-        rz_f[...] += rel_y[d - 1].astype(F32)
-    rz_s[...] = rz_f[...].astype(BF16)
-    z_out = []
+        ya_in[d - 1].wait_recv()
+        total += rel_y[d - 1].astype(F32)
+    ya_f[...] = total
+    ya_s[...] = total.astype(BF16)
+    ya_out = []
     for d in range(1, NZ):
         zp = lax.rem(z + d, NZ)
-        part = rz_s.at[:, pl.ds(pl.multiple_of(zp * 16, 16), 16), :]
-        z_out.append(send(part, rz_r.at[d - 1], z_sem.at[d - 1], z_sem.at[6 + d], b + (zp - z) * NY, r))
+        to = b + (zp - z) * NY
+        ya_out.append(send(ya_s.at[zp], ya_r.at[d - 1], z2_sem.at[d - 1], z2_sem.at[6 + d], to, r))
+    total = rel_f[1, :, z]
+    for d in range(1, NZ):
+        zb_in[d - 1].wait_recv()
+        total += rel_z[d - 1].astype(F32)
+    zb_f[...] = total
+    zb_s[...] = total.astype(BF16)
+    zb_out = []
+    for d in range(1, NY):
+        yp = lax.rem(y + d, NY)
+        zb_out.append(send(zb_s.at[yp], zb_r.at[d - 1], y2_sem.at[d - 1], y2_sem.at[2 + d], b - y + yp, r))
 
     def from_above():
         low_out.wait_recv()
@@ -322,12 +339,18 @@
         rp = lax.rem(r + d, NREP)
         rep_out.append(send(loc_s.at[rp], loc_r.at[d - 1], rep_sem.at[d - 1], rep_sem.at[2 + d], b, rp))
 
-    total = rz_f[:, pl.ds(pl.multiple_of(z * 16, 16), 16), :]
+    total = ya_f[z]
     for d in range(1, NZ):
-        z_out[d - 1].wait_recv()
-        total += rz_r[d - 1].astype(F32)
+        ya_out[d - 1].wait_recv()
+        total += ya_r[d - 1].astype(F32)
     for x in range(NX):
-        rx_s[x] = total[:, x * 8 : (x + 1) * 8, :]
+        rx_s[x, 0] = total[x * 8 : (x + 1) * 8, :]
+    total = zb_f[y]
+    for d in range(1, NY):
+        zb_out[d - 1].wait_recv()
+        total += zb_r[d - 1].astype(F32)
+    for x in range(NX):
+        rx_s[x, 1] = total[x * 8 : (x + 1) * 8, :]
     x_out = send(rx_s.at[xp], rx_r, x_sem.at[4], x_sem.at[5], other_x, r)
     total = loc[r]
     for d in range(1, NREP):
@@ -345,7 +368,7 @@
     pl.when(y <= 1)(down_out.wait_send)
     pl.when(y >= 1)(low_out.wait_send)
     pl.when(y <= 1)(high_out.wait_send)
-    for copy in (*block_out, head_out, *term_out, pair_out, *y_out, *rep_out, *z_out, x_out):
+    for copy in (*block_out, head_out, *term_out, pair_out, *ya_in, *zb_in, *ya_out, *zb_out, *rep_out, x_out):
         copy.wait_send()
     wait_all(asked.at[pl.ds(0, NBLK - 1)], a2a_sem.at[0])
     wait_all(served.at[pl.ds(0, (NBLK - 1) * 16)], a2a_sem.at[2])
@@ -392,12 +415,16 @@
         pltpu.VMEM((2, 256, D), BF16),
         pltpu.VMEM((1024, 256), BF16),
         pltpu.VMEM((1024, 256), BF16),
-        pltpu.VMEM((2, D, D), F32),
-        pltpu.VMEM((2, D, D), BF16),
-        pltpu.VMEM((NY - 1, 2, 128, D), BF16),
-        pltpu.VMEM((2, 128, D), F32),
-        pltpu.VMEM((2, 128, D), BF16),
-        pltpu.VMEM((NZ - 1, 2, 16, D), BF16),
+        pltpu.VMEM((2, NY, NZ, 16, D), F32),
+        pltpu.VMEM((2, NY, NZ, 16, D), BF16),
+        pltpu.VMEM((NY - 1, NZ, 16, D), BF16),
+        pltpu.VMEM((NZ - 1, NY, 16, D), BF16),
+        pltpu.VMEM((NZ, 16, D), F32),
+        pltpu.VMEM((NZ, 16, D), BF16),
+        pltpu.VMEM((NZ - 1, 16, D), BF16),
+        pltpu.VMEM((NY, 16, D), F32),
+        pltpu.VMEM((NY, 16, D), BF16),
+        pltpu.VMEM((NY - 1, 16, D), BF16),
         pltpu.VMEM((NX, 2, 8, D), F32),
         pltpu.VMEM((2, 8, D), F32),
         pltpu.VMEM((4, D, 128), F32),
@@ -409,6 +436,8 @@
         dma((10,)),
         dma((8,)),
         dma((6,)),
+        dma((6,)),
+        dma((14,)),
         dma((6,)),
         dma((14,)),
         dma((6,)),

time: 102 us -> 105 us (1.029)
  the two profiles are of different devices: /device:TPU:16 before, /device:TPU:1 now
where the time goes in v3:
time: 105 us; the launch traced here: 104 us
  Pallas kernels  101 us (96%)
  local copies, waits for them, and re-layouts  3.14 us (3%)
    pallas_call x1, Pallas kernels, per_device(): pl.pallas_call(kernel, out_shape=(jax.ShapeDtypeStruct((D, 128), F32), ja...  101 us
    unnamed x2, local copies, waits for them, and re-layouts  3.14 us

profile of v3, /device:TPU:1, one launch (start us, length us, event | category | flops | bytes accessed | tf_op | source)
XLA Modules:
  0.0 104.4 jit_solution(15210139128408304535)
XLA Ops:
  0.6 100.6 %rescal_step.1 = (f32[512,128]{1,0:T(8,128)}, f32[4,8,512]{2,1,0:T(8,128)}) custom-call(bf16[512,512]{1,0:T(8,128)(2,1)} %ent_h.1, bf16[4,512,512]{2,1,0:T(8,128)(2,1)} %rel_h.1, s32[1,256]{1,0:T(1,128)} %bitcast.6, s32[1,256]{1,0:T(1,128)} %bitcast.7, s32[4,256]{1,0:T(4,128)} %bitcast.4, s32[4,256]{1,0:T(4,128)} %bitcast.5, s32[1,256]{1,0:T(1,128)} %neg_h.1), custom_call_target="tpu_custom_call" | custom-call | tf_op jit(solution)/shard_map/rescal_step/pallas_call | solution.py:445
  101.2 1.7 %copy.11 = f32[512,128]{1,0:T(8,128)} copy(f32[512,128]{1,0:T(8,128)} %get-tuple-element.4) | data formatting | bytes 524288
  102.9 1.5 %copy.12 = f32[4,8,512]{2,1,0:T(8,128)} copy(f32[4,8,512]{2,1,0:T(8,128)} %get-tuple-element.5) | data formatting | bytes 131072

commit v4 on v2

--- a/solution.py
+++ b/solution.py
@@ -45,9 +45,9 @@
 def kernel(
     ent_h, rel_h, owner_h, row_h, kind_h, tail_h, neg_h, out_e, out_r,
     ent, rel, owner_v, row_v, kind_v, tail_v, neg_v, rows, cols, asked, wanted, wanted2, w_row, served, fetched, blocks, relay, tails, head, head_t, head_p,
-    prod, query, pos_w, grad_q, weights, pair, pair_p, term_own, term_s, term_r, term_f, relay_s, relay_r, back_s, back_r,
+    prod, query, pos_w, grad_q, weights, pair, pair_p, term_own, term_s, term_r, near, chain_r, term_f, relay_s, relay_r, back_s, back_r,
     rel_f, rel_s, rel_y, rz_f, rz_s, rz_r, rx_s, rx_r, loc, loc_s, loc_r,
-    in_sem, a2a_sem, nb_sem, gt_sem, hop_sem, x_sem, y_sem, z_sem, rep_sem,
+    in_sem, a2a_sem, nb_sem, gt_sem, chain_sem, hop_sem, x_sem, y_sem, z_sem, rep_sem,
 ):
     b, r = lax.axis_index("blk"), lax.axis_index("rep")
     y, z, xl = lax.rem(b, NY), lax.rem(lax.div(b, NY), NZ), lax.div(b, NY * NZ)
@@ -145,7 +145,8 @@
         sems = nb_sem.at[n - 1], nb_sem.at[4 + n]
         block_out.append(remote(block(0), block(n), *sems, visitor, r))
         block_far.append(remote(relay.at[0 if OFFS[n] > 0 else 1], block(n), *sems, visitor, r))
-        pl.when((y + OFFS[n] >= 0) & (y + OFFS[n] < NY))(block_out[n - 1].start)
+        if abs(OFFS[n]) != 2:
+            pl.when((y + OFFS[n] >= 0) & (y + OFFS[n] < NY))(block_out[n - 1].start)
     for j in range(2):
         tails[j * 256 : (j + 1) * 256] = mm(hot(iota((256, D), 1) == cols[:, 6 + j : 7 + j]), ent[...]).astype(BF16)
     wait_all(wanted.at[pl.ds(0, NBLK - 1)], a2a_sem.at[1])
@@ -166,8 +167,17 @@
     fetched[mine] = served[mine]
     pl.when(y >= 1)(up_out.wait_recv)
     pl.when(y <= 1)(down_out.wait_recv)
-    for n in range(1, STOPS):
+    for n in (1, 2, 5):
         pl.when((y + OFFS[n] < 0) | (y + OFFS[n] >= NY))(block_far[n - 1].start)
+    pl.when(y == 2)(block_far[2].start)
+    pl.when(y == 1)(block_far[3].start)
+    next_y, last_y = b - y + lax.rem(y + 1, NY), b - y + lax.rem(y + NY - 1, NY)
+    on_up = remote(block(1), block(3), chain_sem.at[0], nb_sem.at[7], next_y, r)
+    on_down = remote(block(2), block(4), chain_sem.at[1], nb_sem.at[8], last_y, r)
+    block_out[0].wait_recv()
+    pl.when(y <= 2)(on_up.start)
+    block_out[1].wait_recv()
+    pl.when(y >= 1)(on_down.start)
     for j in range(2, 4):
         tails[j * 256 : (j + 1) * 256] = mm(hot(iota((256, D), 1) == cols[:, 6 + j : 7 + j]), ent[...]).astype(BF16)
     wait_all(fetched.at[pl.ds(0, (NBLK - 1) * 16)], a2a_sem.at[3])
@@ -204,7 +214,7 @@
 
     term_out = []
     for n in range(STOPS):
-        if n:
+        if n > 2:
             block_out[n - 1].wait_recv()
         met = slice(n * 256, (n + 1) * 256)
         weights[:, met] = (jax.nn.sigmoid(mm_nt(query[...], block(n)[...])) * (1.0 / STOPS)).astype(BF16)
@@ -212,9 +222,22 @@
         if n == 0:
             term_own[...] = term
         else:
+            via = b - y + lax.rem(y - OFFS[n] + NY, NY)
+            term_out.append(remote(term_s.at[n - 1], term_r.at[n - 1], gt_sem.at[n - 1], gt_sem.at[4 + n], via, r))
+            if n <= 2:
+                near[n - 1] = term
+                continue
             term_s[n - 1] = term.astype(BF16)
-            via = b - y + lax.rem(y - OFFS[n] + NY, NY)
-            term_out.append(send(term_s.at[n - 1], term_r.at[n - 1], gt_sem.at[n - 1], gt_sem.at[4 + n], via, r))
+            if n == 3:
+                pl.when(y == 0)(term_out[2].start)
+                term_up = remote(term_s.at[2], chain_r.at[0], gt_sem.at[2], chain_sem.at[2], last_y, r)
+                pl.when(y >= 1)(term_up.start)
+            elif n == 4:
+                pl.when(y == 3)(term_out[3].start)
+                term_down = remote(term_s.at[3], chain_r.at[1], gt_sem.at[3], chain_sem.at[3], next_y, r)
+                pl.when(y <= 2)(term_down.start)
+            else:
+                term_out[4].start()
         for upto, since in ((4, 0), (STOPS, 4)):
             if n == upto - 1:
                 met = slice(since * 256, upto * 256)
@@ -246,6 +269,27 @@
     to_all(rows16(back_s), back_r.at[mine], a2a_sem.at[4], a2a_sem.at[5])
     back_r[mine] = back_s[mine]
 
+    for j in range(4):
+        onto = hot(iota((D, 256), 0) == rows[6 + j : 7 + j, :])
+        high, low = two_parts(pos_w[j * 256 : (j + 1) * 256, 0:1] * query[j * 256 : (j + 1) * 256, :].astype(F32))
+        part = mm(onto, high) + mm(onto, low)
+        for c in range(4):
+            loc[c] = part[:, c * 128 : (c + 1) * 128] if j == 0 else loc[c] + part[:, c * 128 : (c + 1) * 128]
+
+    def add_up():
+        term_up.wait_recv()
+        near[0] += chain_r[0].astype(F32)
+
+    def add_down():
+        term_down.wait_recv()
+        near[1] += chain_r[1].astype(F32)
+
+    pl.when(y <= 2)(add_up)
+    pl.when(y >= 1)(add_down)
+    for n in (1, 2):
+        term_s[n - 1] = near[n - 1].astype(BF16)
+        term_out[n - 1].start()
+
     head_out.wait_recv()
     pair_out.wait_recv()
     for k in range(2):
@@ -257,16 +301,8 @@
         part = rel_s.at[:, pl.ds(pl.multiple_of(yp * 128, 128), 128), :]
         y_out.append(send(part, rel_y.at[d - 1], y_sem.at[d - 1], y_sem.at[2 + d], b - y + yp, r))
 
-    for j in range(4):
-        onto = hot(iota((D, 256), 0) == rows[6 + j : 7 + j, :])
-        high, low = two_parts(pos_w[j * 256 : (j + 1) * 256, 0:1] * query[j * 256 : (j + 1) * 256, :].astype(F32))
-        part = mm(onto, high) + mm(onto, low)
-        for c in range(4):
-            loc[c] = part[:, c * 128 : (c + 1) * 128] if j == 0 else loc[c] + part[:, c * 128 : (c + 1) * 128]
-
     term_f[...] = jnp.zeros_like(term_f)
     for n in range(1, STOPS):
-        term_out[n - 1].wait_recv()
 
         def own(n=n):
             term_own[...] += term_r[n - 1].astype(F32)
@@ -274,8 +310,18 @@
         def other(n=n):
             term_f[0 if OFFS[n] > 0 else 1] += term_r[n - 1].astype(F32)
 
-        pl.when((y + OFFS[n] >= 0) & (y + OFFS[n] < NY))(own)
-        pl.when((y + OFFS[n] < 0) | (y + OFFS[n] >= NY))(other)
+        def far(n=n):
+            term_out[n - 1].wait_recv()
+            term_f[0 if OFFS[n] > 0 else 1] += term_r[n - 1].astype(F32)
+
+        if n == 3:
+            pl.when(y == 2)(far)
+        elif n == 4:
+            pl.when(y == 1)(far)
+        else:
+            term_out[n - 1].wait_recv()
+            pl.when((y + OFFS[n] >= 0) & (y + OFFS[n] < NY))(own)
+            pl.when((y + OFFS[n] < 0) | (y + OFFS[n] >= NY))(other)
     relay_s[...] = term_f[...].astype(BF16)
     low_out = remote(relay_s.at[0], relay_r.at[0], hop_sem.at[4], hop_sem.at[5], plane_down, r)
     high_out = remote(relay_s.at[1], relay_r.at[1], hop_sem.at[6], hop_sem.at[7], plane_up, r)
@@ -345,7 +391,11 @@
     pl.when(y <= 1)(down_out.wait_send)
     pl.when(y >= 1)(low_out.wait_send)
     pl.when(y <= 1)(high_out.wait_send)
-    for copy in (*block_out, head_out, *term_out, pair_out, *y_out, *rep_out, *z_out, x_out):
+    pl.when(y == 2)(block_out[2].wait_send)
+    pl.when(y == 1)(block_out[3].wait_send)
+    pl.when(y <= 2)(on_up.wait_send)
+    pl.when(y >= 1)(on_down.wait_send)
+    for copy in (block_out[0], block_out[1], block_out[4], head_out, *term_out, pair_out, *y_out, *rep_out, *z_out, x_out):
         copy.wait_send()
     wait_all(asked.at[pl.ds(0, NBLK - 1)], a2a_sem.at[0])
     wait_all(served.at[pl.ds(0, (NBLK - 1) * 16)], a2a_sem.at[2])
@@ -389,6 +439,8 @@
         pltpu.VMEM((STOPS - 1, 256, D), BF16),
         pltpu.VMEM((2, 256, D), F32),
         pltpu.VMEM((2, 256, D), BF16),
+        pltpu.VMEM((2, 256, D), F32),
+        pltpu.VMEM((2, 256, D), BF16),
         pltpu.VMEM((2, 256, D), BF16),
         pltpu.VMEM((1024, 256), BF16),
         pltpu.VMEM((1024, 256), BF16),
@@ -407,6 +459,7 @@
         dma((6,)),
         dma((10,)),
         dma((10,)),
+        dma((4,)),
         dma((8,)),
         dma((6,)),
         dma((6,)),

time: 102 us -> 106 us (1.039)
  Pallas kernels: 97.7 us -> 102 us
    pallas_call x1, Pallas kernels: 97.7 us -> 102 us  [per_device(): pl.pallas_call(kernel, out_shape=(jax.ShapeDtypeStruct((D, 128), F32), ja...]
where the time goes in v4:
time: 106 us; the launch traced here: 105 us
  Pallas kernels  102 us (96%)
  local copies, waits for them, and re-layouts  3.14 us (3%)
    pallas_call x1, Pallas kernels, per_device(): pl.pallas_call(kernel, out_shape=(jax.ShapeDtypeStruct((D, 128), F32), ja...  102 us
    unnamed x2, local copies, waits for them, and re-layouts  3.14 us

profile of v4, /device:TPU:16, one launch (start us, length us, event | category | flops | bytes accessed | tf_op | source)
XLA Modules:
  0.0 105.4 jit_solution(14933386538282903432)
XLA Ops:
  0.6 101.6 %rescal_step.1 = (f32[512,128]{1,0:T(8,128)}, f32[4,8,512]{2,1,0:T(8,128)}) custom-call(bf16[512,512]{1,0:T(8,128)(2,1)} %ent_h.1, bf16[4,512,512]{2,1,0:T(8,128)(2,1)} %rel_h.1, s32[1,256]{1,0:T(1,128)} %bitcast.6, s32[1,256]{1,0:T(1,128)} %bitcast.7, s32[4,256]{1,0:T(4,128)} %bitcast.4, s32[4,256]{1,0:T(4,128)} %bitcast.5, s32[1,256]{1,0:T(1,128)} %neg_h.1), custom_call_target="tpu_custom_call" | custom-call | tf_op jit(solution)/shard_map/rescal_step/pallas_call | solution.py:469
  102.3 1.7 %copy.11 = f32[512,128]{1,0:T(8,128)} copy(f32[512,128]{1,0:T(8,128)} %get-tuple-element.4) | data formatting | bytes 524288
  104.0 1.5 %copy.12 = f32[4,8,512]{2,1,0:T(8,128)} copy(f32[4,8,512]{2,1,0:T(8,128)} %get-tuple-element.5) | data formatting | bytes 131072

commit v5 on v2

--- a/solution.py
+++ b/solution.py
@@ -188,39 +188,41 @@
                 q = jnp.where(kind[:, 2 + j : 3 + j] == k, prod[k, at, :], q)
             q = q.astype(BF16)
             query[to, :] = q
-            tail = tails[to, :].astype(F32)
-            score = jnp.sum(q.astype(F32) * tail, axis=1, keepdims=True)
-            weight = jax.nn.sigmoid(score) - 1.0
-            grad_q[to, :] = weight * tail
-            pos_w[to, :] = jnp.broadcast_to(weight, (16, 128))
         return carry
 
     lax.fori_loop(0, 16, query_rows, 0, unroll=2)
 
-    c = iota((D, D), 0)
-    natural = (c >> 3 & 1) * 256 + (c >> 4 & 7) * 32 + (c >> 7) * 8 + (c & 7)
-    head_t[...] = mm_nt(hot(iota((D, D), 1) == natural), head[...]).astype(BF16)
-    head_out = send(head_t, head_p, x_sem.at[0], x_sem.at[1], other_x, r)
+    def positive_rows(t, carry):
+        at = pl.ds(pl.multiple_of(t * 32, 32), 32)
+        tail = tails[at, :].astype(F32)
+        score = jnp.sum(query[at, :].astype(F32) * tail, axis=1, keepdims=True)
+        weight = jax.nn.sigmoid(score) - 1.0
+        grad_q[at, :] = weight * tail
+        pos_w[at, :] = jnp.broadcast_to(weight, (32, 128))
+        return carry
 
     term_out = []
-    for n in range(STOPS):
-        if n:
-            block_out[n - 1].wait_recv()
+
+    def visit(n):
         met = slice(n * 256, (n + 1) * 256)
         weights[:, met] = (jax.nn.sigmoid(mm_nt(query[...], block(n)[...])) * (1.0 / STOPS)).astype(BF16)
-        term = mm_tn(weights[:, met], query[...])
-        if n == 0:
-            term_own[...] = term
-        else:
-            term_s[n - 1] = term.astype(BF16)
-            via = b - y + lax.rem(y - OFFS[n] + NY, NY)
-            term_out.append(send(term_s.at[n - 1], term_r.at[n - 1], gt_sem.at[n - 1], gt_sem.at[4 + n], via, r))
-        for upto, since in ((4, 0), (STOPS, 4)):
-            if n == upto - 1:
-                met = slice(since * 256, upto * 256)
-                for j in range(4):
-                    at = slice(j * 256, (j + 1) * 256)
-                    grad_q[at, :] += mm(weights[at, met], blocks[met, :])
+        return mm_tn(weights[:, met], query[...])
+
+    for n in range(1, STOPS):
+        if n == 3:
+            c = iota((D, D), 0)
+            natural = (c >> 3 & 1) * 256 + (c >> 4 & 7) * 32 + (c >> 7) * 8 + (c & 7)
+            head_t[...] = mm_nt(hot(iota((D, D), 1) == natural), head[...]).astype(BF16)
+            head_out = send(head_t, head_p, x_sem.at[0], x_sem.at[1], other_x, r)
+            lax.fori_loop(0, 32, positive_rows, 0, unroll=4)
+            term_own[...] = visit(0)
+        block_out[n - 1].wait_recv()
+        term_s[n - 1] = visit(n).astype(BF16)
+        via = b - y + lax.rem(y - OFFS[n] + NY, NY)
+        term_out.append(send(term_s.at[n - 1], term_r.at[n - 1], gt_sem.at[n - 1], gt_sem.at[4 + n], via, r))
+    for j in range(4):
+        at = slice(j * 256, (j + 1) * 256)
+        grad_q[at, :] += mm(weights[at, :], blocks[...])
 
     def pair_rows(t, carry):
         at = pl.ds(pl.multiple_of(t * 16, 16), 16)

time: 102 us -> 103 us (level)
  no operation moved by 1% of the time
where the time goes in v5:
time: 103 us; the launch traced here: 102 us
  Pallas kernels  97.8 us (95%)
  local copies, waits for them, and re-layouts  3.14 us (3%)
    pallas_call x1, Pallas kernels, per_device(): pl.pallas_call(kernel, out_shape=(jax.ShapeDtypeStruct((D, 128), F32), ja...  97.8 us
    unnamed x2, local copies, waits for them, and re-layouts  3.14 us

profile of v5, /device:TPU:16, one launch (start us, length us, event | category | flops | bytes accessed | tf_op | source)
XLA Modules:
  0.0 101.6 jit_solution(9502585653326927830)
XLA Ops:
  0.6 97.8 %rescal_step.1 = (f32[512,128]{1,0:T(8,128)}, f32[4,8,512]{2,1,0:T(8,128)}) custom-call(bf16[512,512]{1,0:T(8,128)(2,1)} %ent_h.1, bf16[4,512,512]{2,1,0:T(8,128)(2,1)} %rel_h.1, s32[1,256]{1,0:T(1,128)} %bitcast.6, s32[1,256]{1,0:T(1,128)} %bitcast.7, s32[4,256]{1,0:T(4,128)} %bitcast.4, s32[4,256]{1,0:T(4,128)} %bitcast.5, s32[1,256]{1,0:T(1,128)} %neg_h.1), custom_call_target="tpu_custom_call" | custom-call | tf_op jit(solution)/shard_map/rescal_step/pallas_call | solution.py:418
  98.4 1.7 %copy.11 = f32[512,128]{1,0:T(8,128)} copy(f32[512,128]{1,0:T(8,128)} %get-tuple-element.4) | data formatting | bytes 524288
  100.1 1.5 %copy.12 = f32[4,8,512]{2,1,0:T(8,128)} copy(f32[4,8,512]{2,1,0:T(8,128)} %get-tuple-element.5) | data formatting | bytes 131072

commit v6 on v2

--- a/solution.py
+++ b/solution.py
@@ -47,7 +47,7 @@
     ent, rel, owner_v, row_v, kind_v, tail_v, neg_v, rows, cols, asked, wanted, wanted2, w_row, served, fetched, blocks, relay, tails, head, head_t, head_p,
     prod, query, pos_w, grad_q, weights, pair, pair_p, term_own, term_s, term_r, term_f, relay_s, relay_r, back_s, back_r,
     rel_f, rel_s, rel_y, rz_f, rz_s, rz_r, rx_s, rx_r, loc, loc_s, loc_r,
-    in_sem, a2a_sem, nb_sem, gt_sem, hop_sem, x_sem, y_sem, z_sem, rep_sem,
+    in_sem, a2a_sem, nb_sem, chain_sem, gt_sem, hop_sem, x_sem, y_sem, z_sem, rep_sem,
 ):
     b, r = lax.axis_index("blk"), lax.axis_index("rep")
     y, z, xl = lax.rem(b, NY), lax.rem(lax.div(b, NY), NZ), lax.div(b, NY * NZ)
@@ -145,7 +145,8 @@
         sems = nb_sem.at[n - 1], nb_sem.at[4 + n]
         block_out.append(remote(block(0), block(n), *sems, visitor, r))
         block_far.append(remote(relay.at[0 if OFFS[n] > 0 else 1], block(n), *sems, visitor, r))
-        pl.when((y + OFFS[n] >= 0) & (y + OFFS[n] < NY))(block_out[n - 1].start)
+        if abs(OFFS[n]) != 2:
+            pl.when((y + OFFS[n] >= 0) & (y + OFFS[n] < NY))(block_out[n - 1].start)
     for j in range(2):
         tails[j * 256 : (j + 1) * 256] = mm(hot(iota((256, D), 1) == cols[:, 6 + j : 7 + j]), ent[...]).astype(BF16)
     wait_all(wanted.at[pl.ds(0, NBLK - 1)], a2a_sem.at[1])
@@ -166,8 +167,24 @@
     fetched[mine] = served[mine]
     pl.when(y >= 1)(up_out.wait_recv)
     pl.when(y <= 1)(down_out.wait_recv)
-    for n in range(1, STOPS):
+    for n in (1, 2, 5):
         pl.when((y + OFFS[n] < 0) | (y + OFFS[n] >= NY))(block_far[n - 1].start)
+    pl.when(y == 2)(block_far[2].start)
+    pl.when(y == 1)(block_far[3].start)
+    next_y, last_y = b - y + lax.rem(y + 1, NY), b - y + lax.rem(y + NY - 1, NY)
+    on_up = remote(block(1), block(3), chain_sem.at[0], nb_sem.at[7], next_y, r)
+    on_down = remote(block(2), block(4), chain_sem.at[1], nb_sem.at[8], last_y, r)
+
+    def pass_up():
+        block_out[0].wait_recv()
+        on_up.start()
+
+    def pass_down():
+        block_out[1].wait_recv()
+        on_down.start()
+
+    pl.when((y >= 1) & (y <= 2))(pass_up)
+    pl.when((y >= 1) & (y <= 2))(pass_down)
     for j in range(2, 4):
         tails[j * 256 : (j + 1) * 256] = mm(hot(iota((256, D), 1) == cols[:, 6 + j : 7 + j]), ent[...]).astype(BF16)
     wait_all(fetched.at[pl.ds(0, (NBLK - 1) * 16)], a2a_sem.at[3])
@@ -197,6 +214,11 @@
 
     lax.fori_loop(0, 16, query_rows, 0, unroll=2)
 
+    pl.when(y == 0)(pass_up)
+    pl.when(y == 3)(pass_down)
+    pl.when(y == 3)(block_out[0].wait_recv)
+    pl.when(y == 0)(block_out[1].wait_recv)
+
     c = iota((D, D), 0)
     natural = (c >> 3 & 1) * 256 + (c >> 4 & 7) * 32 + (c >> 7) * 8 + (c & 7)
     head_t[...] = mm_nt(hot(iota((D, D), 1) == natural), head[...]).astype(BF16)
@@ -204,7 +226,7 @@
 
     term_out = []
     for n in range(STOPS):
-        if n:
+        if n > 2:
             block_out[n - 1].wait_recv()
         met = slice(n * 256, (n + 1) * 256)
         weights[:, met] = (jax.nn.sigmoid(mm_nt(query[...], block(n)[...])) * (1.0 / STOPS)).astype(BF16)
@@ -345,7 +367,11 @@
     pl.when(y <= 1)(down_out.wait_send)
     pl.when(y >= 1)(low_out.wait_send)
     pl.when(y <= 1)(high_out.wait_send)
-    for copy in (*block_out, head_out, *term_out, pair_out, *y_out, *rep_out, *z_out, x_out):
+    pl.when(y == 2)(block_out[2].wait_send)
+    pl.when(y == 1)(block_out[3].wait_send)
+    pl.when(y <= 2)(on_up.wait_send)
+    pl.when(y >= 1)(on_down.wait_send)
+    for copy in (block_out[0], block_out[1], block_out[4], head_out, *term_out, pair_out, *y_out, *rep_out, *z_out, x_out):
         copy.wait_send()
     wait_all(asked.at[pl.ds(0, NBLK - 1)], a2a_sem.at[0])
     wait_all(served.at[pl.ds(0, (NBLK - 1) * 16)], a2a_sem.at[2])
@@ -406,6 +432,7 @@
         dma((7,)),
         dma((6,)),
         dma((10,)),
+        dma((2,)),
         dma((10,)),
         dma((8,)),
         dma((6,)),

time: 102 us -> 100 us (0.980)
  Pallas kernels: 97.7 us -> 96.5 us
    pallas_call x1, Pallas kernels: 97.7 us -> 96.5 us  [per_device(): pl.pallas_call(kernel, out_shape=(jax.ShapeDtypeStruct((D, 128), F32), ja...]
where the time goes in v6:
time: 100 us
  Pallas kernels  96.5 us (96%)
  local copies, waits for them, and re-layouts  3.14 us (3%)
    pallas_call x1, Pallas kernels, per_device(): pl.pallas_call(kernel, out_shape=(jax.ShapeDtypeStruct((D, 128), F32), ja...  96.5 us
    unnamed x2, local copies, waits for them, and re-layouts  3.14 us

profile of v6, /device:TPU:16, one launch (start us, length us, event | category | flops | bytes accessed | tf_op | source)
XLA Modules:
  0.0 100.2 jit_solution(6158519942630641166)
XLA Ops:
  0.6 96.5 %rescal_step.1 = (f32[512,128]{1,0:T(8,128)}, f32[4,8,512]{2,1,0:T(8,128)}) custom-call(bf16[512,512]{1,0:T(8,128)(2,1)} %ent_h.1, bf16[4,512,512]{2,1,0:T(8,128)(2,1)} %rel_h.1, s32[1,256]{1,0:T(1,128)} %bitcast.6, s32[1,256]{1,0:T(1,128)} %bitcast.7, s32[4,256]{1,0:T(4,128)} %bitcast.4, s32[4,256]{1,0:T(4,128)} %bitcast.5, s32[1,256]{1,0:T(1,128)} %neg_h.1), custom_call_target="tpu_custom_call" | custom-call | tf_op jit(solution)/shard_map/rescal_step/pallas_call | solution.py:443
  97.1 1.7 %copy.11 = f32[512,128]{1,0:T(8,128)} copy(f32[512,128]{1,0:T(8,128)} %get-tuple-element.4) | data formatting | bytes 524288
  98.8 1.5 %copy.12 = f32[4,8,512]{2,1,0:T(8,128)} copy(f32[4,8,512]{2,1,0:T(8,128)} %get-tuple-element.5) | data formatting | bytes 131072
